TPU v7x, 256 devices: a whole 4x4x8 slice. The times are simulated.
256 devices in a mesh: dp: 16 (over x_lo, y, core), ctx: 16 (over x_hi, z).
Axes of the slice: x: 4 (x_hi: 2, x_lo: 2; x = x_hi * 2 + x_lo), y: 4, z: 8, core: 2. Of those that a mesh axis runs over, the one named last changes fastest.
Arguments:
- query_rows: bfloat16 [65536, 1024], P(('dp', 'ctx')), parts along dimension 0, may hold values from -8 to 8
- key_rows: bfloat16 [65536, 128], P(('dp', 'ctx')), parts along dimension 0, may hold values from -8 to 8
- value_rows: bfloat16 [65536, 128], P(('dp', 'ctx')), parts along dimension 0, may hold values from -6 to 6
- out_grad: bfloat16 [65536, 1024], P(('dp', 'ctx')), parts along dimension 0, may hold values from -6 to 6
- doc_lengths: int32 [256], P('dp'), parts along dimension 0, may hold values from 1 to 1024, as said below
Outputs:
- query_grad: bfloat16 [65536, 1024], P(('dp', 'ctx')), parts along dimension 0
- key_grad: bfloat16 [65536, 128], P(('dp', 'ctx')), parts along dimension 0
- value_grad: bfloat16 [65536, 128], P(('dp', 'ctx')), parts along dimension 0
There are 16 independent parts, one for each index of `dp`. A program takes and returns all parts, laid end to end along the dimension named above; each array names one. Nothing has to cross between parts.
Inputs may be any that keep to these rules, and one draw needn't show every extreme that they name: `doc_lengths`: the lengths sum to 4096, and the first of them is exactly 1024.
All inputs are finite; a program needn't handle non-finite values.
Results may differ from a plain program's by a relative error of at most 0.0071.
Values may be sent and summed in bfloat16 or wider, within the bound.
A program may use at most 64 MiB of HBM per device.

v0:
```python
import math

import jax
import jax.numpy as jnp
from jax import lax
from jax.sharding import PartitionSpec as P

masked_value = -1e30


def shifted(value, axis, by):
    size = lax.axis_size(axis)
    pairs = [(i, i + by) for i in range(size) if 0 <= i + by < size]
    return lax.ppermute(value, axis, pairs)


def passed_along(block, axis, distance):
    devices = range(lax.axis_size(axis))
    route = [((i - distance) % len(devices), i) for i in devices]
    return lax.ppermute(block, axis, route)


def doc_numbers(positions, doc_ends):
    return jnp.sum((positions[:, None] >= doc_ends[None, :]).astype(jnp.int32), axis=1)


def shards(query_rows, key_rows, value_rows, out_grad, doc_lengths):
    cycle_size = lax.axis_size("ctx")
    own_index = lax.axis_index("ctx")
    shard_rows = query_rows.shape[0]
    head_width = key_rows.shape[1]
    head_count = query_rows.shape[1] // head_width
    score_scale = 1.0 / math.sqrt(head_width)
    doc_ends = jnp.cumsum(doc_lengths)
    query_first = own_index * shard_rows
    query_places = query_first + jnp.arange(shard_rows, dtype=jnp.int32)
    query_docs = doc_numbers(query_places, doc_ends)
    queries = query_rows.reshape(shard_rows, head_count, head_width)
    grads_out = out_grad.reshape(shard_rows, head_count, head_width)

    def pair_mask(key_start, key_count):
        key_places = key_start + jnp.arange(key_count, dtype=jnp.int32)
        key_docs = doc_numbers(key_places, doc_ends)
        allowed = (
            (query_docs[:, None] == key_docs[None, :])
            & (key_places[None, :] <= query_places[:, None])
        )[:, None, :]
        useful = (key_start <= query_first + shard_rows - 1) & (
            key_docs[key_count - 1] >= query_docs[0]
        )
        return (allowed, useful)

    def scores_of(kv_block, allowed):
        raw_scores = (
            jnp.einsum("thd,sd->ths", queries, kv_block[0], preferred_element_type=jnp.float32)
            * score_scale
        )
        masked = jnp.where(allowed, raw_scores, masked_value)
        grad_dots = jnp.einsum(
            "thd,sd->ths", grads_out, kv_block[1], preferred_element_type=jnp.float32
        )
        return (masked, grad_dots)

    def stats_add(row_stats, kv_block, key_start):
        allowed, useful = pair_mask(key_start, kv_block.shape[1])

        def stats_compute(previous):
            row_top, row_total, weighted = previous
            masked, grad_dots = scores_of(kv_block, allowed)
            fresh_top = jnp.maximum(row_top, jnp.max(masked, axis=2))
            rescale = jnp.exp(row_top - fresh_top)
            exp_terms = jnp.where(allowed, jnp.exp(masked - fresh_top[:, :, None]), 0.0)
            return (
                fresh_top,
                row_total * rescale + jnp.sum(exp_terms, axis=2),
                weighted * rescale + jnp.sum(exp_terms * grad_dots, axis=2),
            )

        return lax.cond(useful, stats_compute, lambda previous: previous, row_stats)

    def grads_add(state, kv_block, key_start, log_total, row_delta):
        allowed, useful = pair_mask(key_start, kv_block.shape[1])

        def grads_compute(previous):
            query_acc, kv_acc = previous
            masked, grad_dots = scores_of(kv_block, allowed)
            softmax = jnp.exp(masked - log_total[:, :, None])
            score_grad = softmax * (grad_dots - row_delta[:, :, None])
            soft_low = softmax.astype(jnp.bfloat16)
            grad_low = score_grad.astype(jnp.bfloat16)
            value_part = jnp.einsum(
                "ths,thd->sd", soft_low, grads_out, preferred_element_type=jnp.float32
            )
            key_part = (
                jnp.einsum("ths,thd->sd", grad_low, queries, preferred_element_type=jnp.float32)
                * score_scale
            )
            query_part = (
                jnp.einsum("ths,sd->thd", grad_low, kv_block[0], preferred_element_type=jnp.float32)
                * score_scale
            )
            return (query_acc + query_part, kv_acc + jnp.stack([key_part, value_part]))

        return lax.cond(useful, grads_compute, lambda previous: previous, state)

    kv_pair = jnp.stack([key_rows, value_rows])
    start_stats = (
        jnp.full((shard_rows, head_count), masked_value, jnp.float32),
        jnp.zeros((shard_rows, head_count), jnp.float32),
        jnp.zeros((shard_rows, head_count), jnp.float32),
    )
    zeros_query = jnp.zeros((shard_rows, head_count, head_width), jnp.float32)
    zeros_kv = jnp.zeros((2, shard_rows, head_width), jnp.float32)

    def fwd_travel(travel, state):
        moving, row_stats = state
        moving = shifted(moving, "ctx", 1)
        source = (own_index - travel) % cycle_size
        return (moving, stats_add(row_stats, moving, source * shard_rows))

    first_stats = stats_add(start_stats, kv_pair, query_first)
    moved, row_stats = lax.fori_loop(1, cycle_size, fwd_travel, (kv_pair, first_stats))
    row_top, row_total, weighted = row_stats
    log_total = row_top + jnp.log(row_total)
    row_delta = weighted / row_total

    def bwd_travel(travel, state):
        moving, carried, query_acc = state
        source = (own_index - travel) % cycle_size
        query_acc, carried = grads_add(
            (query_acc, carried), moving, source * shard_rows, log_total, row_delta
        )
        moving = shifted(moving, "ctx", 1)
        carried = passed_along(carried, "ctx", 1)
        return (moving, carried, query_acc)

    moved, kv_grads, query_acc = lax.fori_loop(
        0, cycle_size, bwd_travel, (kv_pair, zeros_kv, zeros_query)
    )
    query_grad = query_acc.reshape(shard_rows, head_count * head_width).astype(jnp.bfloat16)
    return (query_grad, kv_grads[0].astype(jnp.bfloat16), kv_grads[1].astype(jnp.bfloat16))


def solution(mesh):
    placed = (
        P(("dp", "ctx"), None),
        P(("dp", "ctx"), None),
        P(("dp", "ctx"), None),
        P(("dp", "ctx"), None),
        P("dp"),
    )
    return jax.shard_map(
        shards,
        mesh=mesh,
        in_specs=placed,
        out_specs=(P(("dp", "ctx"), None), P(("dp", "ctx"), None), P(("dp", "ctx"), None)),
        check_vma=False,
    )
```

profile of v0, /device:TPU:22, one launch (start us, length us, event | category | flops | bytes accessed | tf_op | source)
XLA Modules:
  0.0 430.9 jit_solution(14646361375830176968)
XLA Ops:
  10.5 166.6 %while.42 = (s32[]{:T(128)}, bf16[2,256,128]{2,1,0:T(8,128)(2,1)S(1)}, f32[256,8]{0,1:T(8,128)}, f32[256,8]{0,1:T(8,128)S(1)}, f32[256,8]{0,1:T(8,128)S(1)}, /*i...) while((s32[]{:T(128)}, ...), condition=%wide.region_14.15_spmd.clone, body=%wide.region_7.14_spmd.clone.sunk | while | flops 275991072 | bytes 8681048 | solution.py:122
  31.1 6.0 %collective-permute-done = bf16[2,256,128]{2,1,0:T(8,128)(2,1)S(1)} collective-permute-done((bf16[2,256,128]{2,1,0:T(8,128)(2,1)S(1)}, bf16[2,256,128]{2,1,0:T(8,128)(2,1)S(1)}, u32[]{:S(2)}, u32[]{:S(2)}) %collective-permute-start) | collective-permute-done | bytes 131104 | tf_op jit(solution)/shard_map/while/body/eval_jaxpr/ppermute | solution.py:14
  41.6 6.0 %collective-permute-done = bf16[2,256,128]{2,1,0:T(8,128)(2,1)S(1)} collective-permute-done((bf16[2,256,128]{2,1,0:T(8,128)(2,1)S(1)}, bf16[2,256,128]{2,1,0:T(8,128)(2,1)S(1)}, u32[]{:S(2)}, u32[]{:S(2)}) %collective-permute-start) | collective-permute-done | bytes 131104 | tf_op jit(solution)/shard_map/while/body/eval_jaxpr/ppermute | solution.py:14
  52.1 6.0 %collective-permute-done = bf16[2,256,128]{2,1,0:T(8,128)(2,1)S(1)} collective-permute-done((bf16[2,256,128]{2,1,0:T(8,128)(2,1)S(1)}, bf16[2,256,128]{2,1,0:T(8,128)(2,1)S(1)}, u32[]{:S(2)}, u32[]{:S(2)}) %collective-permute-start) | collective-permute-done | bytes 131104 | tf_op jit(solution)/shard_map/while/body/eval_jaxpr/ppermute | solution.py:14
  62.6 6.0 %collective-permute-done = bf16[2,256,128]{2,1,0:T(8,128)(2,1)S(1)} collective-permute-done((bf16[2,256,128]{2,1,0:T(8,128)(2,1)S(1)}, bf16[2,256,128]{2,1,0:T(8,128)(2,1)S(1)}, u32[]{:S(2)}, u32[]{:S(2)}) %collective-permute-start) | collective-permute-done | bytes 131104 | tf_op jit(solution)/shard_map/while/body/eval_jaxpr/ppermute | solution.py:14
  73.1 6.0 %collective-permute-done = bf16[2,256,128]{2,1,0:T(8,128)(2,1)S(1)} collective-permute-done((bf16[2,256,128]{2,1,0:T(8,128)(2,1)S(1)}, bf16[2,256,128]{2,1,0:T(8,128)(2,1)S(1)}, u32[]{:S(2)}, u32[]{:S(2)}) %collective-permute-start) | collective-permute-done | bytes 131104 | tf_op jit(solution)/shard_map/while/body/eval_jaxpr/ppermute | solution.py:14
  83.6 6.0 %collective-permute-done = bf16[2,256,128]{2,1,0:T(8,128)(2,1)S(1)} collective-permute-done((bf16[2,256,128]{2,1,0:T(8,128)(2,1)S(1)}, bf16[2,256,128]{2,1,0:T(8,128)(2,1)S(1)}, u32[]{:S(2)}, u32[]{:S(2)}) %collective-permute-start) | collective-permute-done | bytes 131104 | tf_op jit(solution)/shard_map/while/body/eval_jaxpr/ppermute | solution.py:14
  94.1 6.7 %collective-permute-done = bf16[2,256,128]{2,1,0:T(8,128)(2,1)S(1)} collective-permute-done((bf16[2,256,128]{2,1,0:T(8,128)(2,1)S(1)}, bf16[2,256,128]{2,1,0:T(8,128)(2,1)S(1)}, u32[]{:S(2)}, u32[]{:S(2)}) %collective-permute-start) | collective-permute-done | bytes 131104 | tf_op jit(solution)/shard_map/while/body/eval_jaxpr/ppermute | solution.py:14
  105.3 7.0 %collective-permute-done = bf16[2,256,128]{2,1,0:T(8,128)(2,1)S(1)} collective-permute-done((bf16[2,256,128]{2,1,0:T(8,128)(2,1)S(1)}, bf16[2,256,128]{2,1,0:T(8,128)(2,1)S(1)}, u32[]{:S(2)}, u32[]{:S(2)}) %collective-permute-start) | collective-permute-done | bytes 131104 | tf_op jit(solution)/shard_map/while/body/eval_jaxpr/ppermute | solution.py:14
  116.8 6.3 %collective-permute-done = bf16[2,256,128]{2,1,0:T(8,128)(2,1)S(1)} collective-permute-done((bf16[2,256,128]{2,1,0:T(8,128)(2,1)S(1)}, bf16[2,256,128]{2,1,0:T(8,128)(2,1)S(1)}, u32[]{:S(2)}, u32[]{:S(2)}) %collective-permute-start) | collective-permute-done | bytes 131104 | tf_op jit(solution)/shard_map/while/body/eval_jaxpr/ppermute | solution.py:14
  127.5 6.0 %collective-permute-done = bf16[2,256,128]{2,1,0:T(8,128)(2,1)S(1)} collective-permute-done((bf16[2,256,128]{2,1,0:T(8,128)(2,1)S(1)}, bf16[2,256,128]{2,1,0:T(8,128)(2,1)S(1)}, u32[]{:S(2)}, u32[]{:S(2)}) %collective-permute-start) | collective-permute-done | bytes 131104 | tf_op jit(solution)/shard_map/while/body/eval_jaxpr/ppermute | solution.py:14
  138.1 6.0 %collective-permute-done = bf16[2,256,128]{2,1,0:T(8,128)(2,1)S(1)} collective-permute-done((bf16[2,256,128]{2,1,0:T(8,128)(2,1)S(1)}, bf16[2,256,128]{2,1,0:T(8,128)(2,1)S(1)}, u32[]{:S(2)}, u32[]{:S(2)}) %collective-permute-start) | collective-permute-done | bytes 131104 | tf_op jit(solution)/shard_map/while/body/eval_jaxpr/ppermute | solution.py:14
  148.6 6.0 %collective-permute-done = bf16[2,256,128]{2,1,0:T(8,128)(2,1)S(1)} collective-permute-done((bf16[2,256,128]{2,1,0:T(8,128)(2,1)S(1)}, bf16[2,256,128]{2,1,0:T(8,128)(2,1)S(1)}, u32[]{:S(2)}, u32[]{:S(2)}) %collective-permute-start) | collective-permute-done | bytes 131104 | tf_op jit(solution)/shard_map/while/body/eval_jaxpr/ppermute | solution.py:14
  159.1 6.0 %collective-permute-done = bf16[2,256,128]{2,1,0:T(8,128)(2,1)S(1)} collective-permute-done((bf16[2,256,128]{2,1,0:T(8,128)(2,1)S(1)}, bf16[2,256,128]{2,1,0:T(8,128)(2,1)S(1)}, u32[]{:S(2)}, u32[]{:S(2)}) %collective-permute-start) | collective-permute-done | bytes 131104 | tf_op jit(solution)/shard_map/while/body/eval_jaxpr/ppermute | solution.py:14
  169.6 7.5 %collective-permute-done = bf16[2,256,128]{2,1,0:T(8,128)(2,1)S(1)} collective-permute-done((bf16[2,256,128]{2,1,0:T(8,128)(2,1)S(1)}, bf16[2,256,128]{2,1,0:T(8,128)(2,1)S(1)}, u32[]{:S(2)}, u32[]{:S(2)}) %collective-permute-start) | collective-permute-done | bytes 131104 | tf_op jit(solution)/shard_map/while/body/eval_jaxpr/ppermute | solution.py:14
  178.0 251.4 %while.43 = (s32[]{:T(128)}, bf16[2,256,128]{2,1,0:T(8,128)(2,1)S(1)}, f32[2,256,128]{2,1,0:T(8,128)S(1)}, f32[256,8,128]{2,0,1:T(8,128)S(1)}, s32[]{:T(128)}, /...) while((s32[]{:T(128)}, ...), condition=%wide.region_19.20_spmd.clone, body=%wide.region_15.19_spmd.clone.sunk | while | flops 675656192 | bytes 17397376 | solution.py:137
  185.4 10.7 %collective-permute-done.2 = f32[2,256,128]{2,1,0:T(8,128)S(1)} collective-permute-done((f32[2,256,128]{2,1,0:T(8,128)S(1)}, f32[2,256,128]{2,1,0:T(8,128)S(1)}, u32[]{:S(2)}, u32[]{:S(2)}) %collective-permute-start.2) | collective-permute-done | bytes 262176 | tf_op jit(solution)/shard_map/while/body/eval_jaxpr/ppermute | solution.py:20
  205.0 8.0 %collective-permute-done.2 = f32[2,256,128]{2,1,0:T(8,128)S(1)} collective-permute-done((f32[2,256,128]{2,1,0:T(8,128)S(1)}, f32[2,256,128]{2,1,0:T(8,128)S(1)}, u32[]{:S(2)}, u32[]{:S(2)}) %collective-permute-start.2) | collective-permute-done | bytes 262176 | tf_op jit(solution)/shard_map/while/body/eval_jaxpr/ppermute | solution.py:20
  219.1 8.0 %collective-permute-done.2 = f32[2,256,128]{2,1,0:T(8,128)S(1)} collective-permute-done((f32[2,256,128]{2,1,0:T(8,128)S(1)}, f32[2,256,128]{2,1,0:T(8,128)S(1)}, u32[]{:S(2)}, u32[]{:S(2)}) %collective-permute-start.2) | collective-permute-done | bytes 262176 | tf_op jit(solution)/shard_map/while/body/eval_jaxpr/ppermute | solution.py:20
  233.2 8.0 %collective-permute-done.2 = f32[2,256,128]{2,1,0:T(8,128)S(1)} collective-permute-done((f32[2,256,128]{2,1,0:T(8,128)S(1)}, f32[2,256,128]{2,1,0:T(8,128)S(1)}, u32[]{:S(2)}, u32[]{:S(2)}) %collective-permute-start.2) | collective-permute-done | bytes 262176 | tf_op jit(solution)/shard_map/while/body/eval_jaxpr/ppermute | solution.py:20
  247.2 8.0 %collective-permute-done.2 = f32[2,256,128]{2,1,0:T(8,128)S(1)} collective-permute-done((f32[2,256,128]{2,1,0:T(8,128)S(1)}, f32[2,256,128]{2,1,0:T(8,128)S(1)}, u32[]{:S(2)}, u32[]{:S(2)}) %collective-permute-start.2) | collective-permute-done | bytes 262176 | tf_op jit(solution)/shard_map/while/body/eval_jaxpr/ppermute | solution.py:20
  261.3 8.0 %collective-permute-done.2 = f32[2,256,128]{2,1,0:T(8,128)S(1)} collective-permute-done((f32[2,256,128]{2,1,0:T(8,128)S(1)}, f32[2,256,128]{2,1,0:T(8,128)S(1)}, u32[]{:S(2)}, u32[]{:S(2)}) %collective-permute-start.2) | collective-permute-done | bytes 262176 | tf_op jit(solution)/shard_map/while/body/eval_jaxpr/ppermute | solution.py:20
  276.4 8.7 %collective-permute-done.2 = f32[2,256,128]{2,1,0:T(8,128)S(1)} collective-permute-done((f32[2,256,128]{2,1,0:T(8,128)S(1)}, f32[2,256,128]{2,1,0:T(8,128)S(1)}, u32[]{:S(2)}, u32[]{:S(2)}) %collective-permute-start.2) | collective-permute-done | bytes 262176 | tf_op jit(solution)/shard_map/while/body/eval_jaxpr/ppermute | solution.py:20
  292.6 9.9 %collective-permute-done.2 = f32[2,256,128]{2,1,0:T(8,128)S(1)} collective-permute-done((f32[2,256,128]{2,1,0:T(8,128)S(1)}, f32[2,256,128]{2,1,0:T(8,128)S(1)}, u32[]{:S(2)}, u32[]{:S(2)}) %collective-permute-start.2) | collective-permute-done | bytes 262176 | tf_op jit(solution)/shard_map/while/body/eval_jaxpr/ppermute | solution.py:20
  310.0 10.8 %collective-permute-done.2 = f32[2,256,128]{2,1,0:T(8,128)S(1)} collective-permute-done((f32[2,256,128]{2,1,0:T(8,128)S(1)}, f32[2,256,128]{2,1,0:T(8,128)S(1)}, u32[]{:S(2)}, u32[]{:S(2)}) %collective-permute-start.2) | collective-permute-done | bytes 262176 | tf_op jit(solution)/shard_map/while/body/eval_jaxpr/ppermute | solution.py:20
  328.1 10.9 %collective-permute-done.2 = f32[2,256,128]{2,1,0:T(8,128)S(1)} collective-permute-done((f32[2,256,128]{2,1,0:T(8,128)S(1)}, f32[2,256,128]{2,1,0:T(8,128)S(1)}, u32[]{:S(2)}, u32[]{:S(2)}) %collective-permute-start.2) | collective-permute-done | bytes 262176 | tf_op jit(solution)/shard_map/while/body/eval_jaxpr/ppermute | solution.py:20
  345.3 10.3 %collective-permute-done.2 = f32[2,256,128]{2,1,0:T(8,128)S(1)} collective-permute-done((f32[2,256,128]{2,1,0:T(8,128)S(1)}, f32[2,256,128]{2,1,0:T(8,128)S(1)}, u32[]{:S(2)}, u32[]{:S(2)}) %collective-permute-start.2) | collective-permute-done | bytes 262176 | tf_op jit(solution)/shard_map/while/body/eval_jaxpr/ppermute | solution.py:20
  361.7 9.4 %collective-permute-done.2 = f32[2,256,128]{2,1,0:T(8,128)S(1)} collective-permute-done((f32[2,256,128]{2,1,0:T(8,128)S(1)}, f32[2,256,128]{2,1,0:T(8,128)S(1)}, u32[]{:S(2)}, u32[]{:S(2)}) %collective-permute-start.2) | collective-permute-done | bytes 262176 | tf_op jit(solution)/shard_map/while/body/eval_jaxpr/ppermute | solution.py:20
  377.2 8.5 %collective-permute-done.2 = f32[2,256,128]{2,1,0:T(8,128)S(1)} collective-permute-done((f32[2,256,128]{2,1,0:T(8,128)S(1)}, f32[2,256,128]{2,1,0:T(8,128)S(1)}, u32[]{:S(2)}, u32[]{:S(2)}) %collective-permute-start.2) | collective-permute-done | bytes 262176 | tf_op jit(solution)/shard_map/while/body/eval_jaxpr/ppermute | solution.py:20
  391.7 8.0 %collective-permute-done.2 = f32[2,256,128]{2,1,0:T(8,128)S(1)} collective-permute-done((f32[2,256,128]{2,1,0:T(8,128)S(1)}, f32[2,256,128]{2,1,0:T(8,128)S(1)}, u32[]{:S(2)}, u32[]{:S(2)}) %collective-permute-start.2) | collective-permute-done | bytes 262176 | tf_op jit(solution)/shard_map/while/body/eval_jaxpr/ppermute | solution.py:20
  405.8 8.0 %collective-permute-done.2 = f32[2,256,128]{2,1,0:T(8,128)S(1)} collective-permute-done((f32[2,256,128]{2,1,0:T(8,128)S(1)}, f32[2,256,128]{2,1,0:T(8,128)S(1)}, u32[]{:S(2)}, u32[]{:S(2)}) %collective-permute-start.2) | collective-permute-done | bytes 262176 | tf_op jit(solution)/shard_map/while/body/eval_jaxpr/ppermute | solution.py:20
  419.9 8.0 %collective-permute-done.2 = f32[2,256,128]{2,1,0:T(8,128)S(1)} collective-permute-done((f32[2,256,128]{2,1,0:T(8,128)S(1)}, f32[2,256,128]{2,1,0:T(8,128)S(1)}, u32[]{:S(2)}, u32[]{:S(2)}) %collective-permute-start.2) | collective-permute-done | bytes 262176 | tf_op jit(solution)/shard_map/while/body/eval_jaxpr/ppermute | solution.py:20
  (388 shorter events, 169.5 us)
Async XLA Ops:
  10.6 12.1 %collective-permute-start = (bf16[2,256,128]{2,1,0:T(8,128)(2,1)S(1)}, bf16[2,256,128]{2,1,0:T(8,128)(2,1)S(1)}, u32[]{:S(2)}, u32[]{:S(2)}) collective-permute-start(bf16[2,256,128]{2,1,0:T(8,128)(2,1)S(1)} %get-tuple-element.1173), channel_id=1, source_target_pairs={{0,1},{1,2},{2,3},{3,4},{4,5},{5,6},{6,7},{7,8},{8,9},{9,10},{10,1... | collective-permute-start | bytes 393224 | tf_op jit(solution)/shard_map/while/body/eval_jaxpr/ppermute | solution.py:14
  26.6 10.5 %collective-permute-start = (bf16[2,256,128]{2,1,0:T(8,128)(2,1)S(1)}, bf16[2,256,128]{2,1,0:T(8,128)(2,1)S(1)}, u32[]{:S(2)}, u32[]{:S(2)}) collective-permute-start(bf16[2,256,128]{2,1,0:T(8,128)(2,1)S(1)} %get-tuple-element.1173), channel_id=1, source_target_pairs={{0,1},{1,2},{2,3},{3,4},{4,5},{5,6},{6,7},{7,8},{8,9},{9,10},{10,1... | collective-permute-start | bytes 393224 | tf_op jit(solution)/shard_map/while/body/eval_jaxpr/ppermute | solution.py:14
  37.1 10.5 %collective-permute-start = (bf16[2,256,128]{2,1,0:T(8,128)(2,1)S(1)}, bf16[2,256,128]{2,1,0:T(8,128)(2,1)S(1)}, u32[]{:S(2)}, u32[]{:S(2)}) collective-permute-start(bf16[2,256,128]{2,1,0:T(8,128)(2,1)S(1)} %get-tuple-element.1173), channel_id=1, source_target_pairs={{0,1},{1,2},{2,3},{3,4},{4,5},{5,6},{6,7},{7,8},{8,9},{9,10},{10,1... | collective-permute-start | bytes 393224 | tf_op jit(solution)/shard_map/while/body/eval_jaxpr/ppermute | solution.py:14
  79.2 10.5 %collective-permute-start = (bf16[2,256,128]{2,1,0:T(8,128)(2,1)S(1)}, bf16[2,256,128]{2,1,0:T(8,128)(2,1)S(1)}, u32[]{:S(2)}, u32[]{:S(2)}) collective-permute-start(bf16[2,256,128]{2,1,0:T(8,128)(2,1)S(1)} %get-tuple-element.1173), channel_id=1, source_target_pairs={{0,1},{1,2},{2,3},{3,4},{4,5},{5,6},{6,7},{7,8},{8,9},{9,10},{10,1... | collective-permute-start | bytes 393224 | tf_op jit(solution)/shard_map/while/body/eval_jaxpr/ppermute | solution.py:14
  89.7 11.1 %collective-permute-start = (bf16[2,256,128]{2,1,0:T(8,128)(2,1)S(1)}, bf16[2,256,128]{2,1,0:T(8,128)(2,1)S(1)}, u32[]{:S(2)}, u32[]{:S(2)}) collective-permute-start(bf16[2,256,128]{2,1,0:T(8,128)(2,1)S(1)} %get-tuple-element.1173), channel_id=1, source_target_pairs={{0,1},{1,2},{2,3},{3,4},{4,5},{5,6},{6,7},{7,8},{8,9},{9,10},{10,1... | collective-permute-start | bytes 393224 | tf_op jit(solution)/shard_map/while/body/eval_jaxpr/ppermute | solution.py:14
  100.9 11.5 %collective-permute-start = (bf16[2,256,128]{2,1,0:T(8,128)(2,1)S(1)}, bf16[2,256,128]{2,1,0:T(8,128)(2,1)S(1)}, u32[]{:S(2)}, u32[]{:S(2)}) collective-permute-start(bf16[2,256,128]{2,1,0:T(8,128)(2,1)S(1)} %get-tuple-element.1173), channel_id=1, source_target_pairs={{0,1},{1,2},{2,3},{3,4},{4,5},{5,6},{6,7},{7,8},{8,9},{9,10},{10,1... | collective-permute-start | bytes 393224 | tf_op jit(solution)/shard_map/while/body/eval_jaxpr/ppermute | solution.py:14
  112.4 10.7 %collective-permute-start = (bf16[2,256,128]{2,1,0:T(8,128)(2,1)S(1)}, bf16[2,256,128]{2,1,0:T(8,128)(2,1)S(1)}, u32[]{:S(2)}, u32[]{:S(2)}) collective-permute-start(bf16[2,256,128]{2,1,0:T(8,128)(2,1)S(1)} %get-tuple-element.1173), channel_id=1, source_target_pairs={{0,1},{1,2},{2,3},{3,4},{4,5},{5,6},{6,7},{7,8},{8,9},{9,10},{10,1... | collective-permute-start | bytes 393224 | tf_op jit(solution)/shard_map/while/body/eval_jaxpr/ppermute | solution.py:14
  165.2 11.9 %collective-permute-start = (bf16[2,256,128]{2,1,0:T(8,128)(2,1)S(1)}, bf16[2,256,128]{2,1,0:T(8,128)(2,1)S(1)}, u32[]{:S(2)}, u32[]{:S(2)}) collective-permute-start(bf16[2,256,128]{2,1,0:T(8,128)(2,1)S(1)} %get-tuple-element.1173), channel_id=1, source_target_pairs={{0,1},{1,2},{2,3},{3,4},{4,5},{5,6},{6,7},{7,8},{8,9},{9,10},{10,1... | collective-permute-start | bytes 393224 | tf_op jit(solution)/shard_map/while/body/eval_jaxpr/ppermute | solution.py:14
  183.4 12.8 %collective-permute-start.2 = (f32[2,256,128]{2,1,0:T(8,128)S(1)}, f32[2,256,128]{2,1,0:T(8,128)S(1)}, u32[]{:S(2)}, u32[]{:S(2)}) collective-permute-start(f32[2,256,128]{2,1,0:T(8,128)S(1)} %get-tuple-element.1137), channel_id=1, source_target_pairs={{15,0},{0,1},{1,2},{2,3},{3,4},{4,5},{5,6},{6,7},{7,8},{8,9},{9,10... | collective-permute-start | bytes 786440 | tf_op jit(solution)/shard_map/while/body/eval_jaxpr/ppermute | solution.py:20
  183.5 14.1 %collective-permute-start.1 = (bf16[2,256,128]{2,1,0:T(8,128)(2,1)S(1)}, bf16[2,256,128]{2,1,0:T(8,128)(2,1)S(1)}, u32[]{:S(2)}, u32[]{:S(2)}) collective-permute-start(bf16[2,256,128]{2,1,0:T(8,128)(2,1)S(1)} %copy.78), channel_id=1, source_target_pairs={{0,1},{1,2},{2,3},{3,4},{4,5},{5,6},{6,7},{7,8},{8,9},{9,10},{10,1... | collective-permute-start | bytes 393224 | tf_op jit(solution)/shard_map/while/body/eval_jaxpr/ppermute | solution.py:14
  203.0 11.4 %collective-permute-start.1 = (bf16[2,256,128]{2,1,0:T(8,128)(2,1)S(1)}, bf16[2,256,128]{2,1,0:T(8,128)(2,1)S(1)}, u32[]{:S(2)}, u32[]{:S(2)}) collective-permute-start(bf16[2,256,128]{2,1,0:T(8,128)(2,1)S(1)} %copy.78), channel_id=1, source_target_pairs={{0,1},{1,2},{2,3},{3,4},{4,5},{5,6},{6,7},{7,8},{8,9},{9,10},{10,1... | collective-permute-start | bytes 393224 | tf_op jit(solution)/shard_map/while/body/eval_jaxpr/ppermute | solution.py:14
  217.1 11.4 %collective-permute-start.1 = (bf16[2,256,128]{2,1,0:T(8,128)(2,1)S(1)}, bf16[2,256,128]{2,1,0:T(8,128)(2,1)S(1)}, u32[]{:S(2)}, u32[]{:S(2)}) collective-permute-start(bf16[2,256,128]{2,1,0:T(8,128)(2,1)S(1)} %copy.78), channel_id=1, source_target_pairs={{0,1},{1,2},{2,3},{3,4},{4,5},{5,6},{6,7},{7,8},{8,9},{9,10},{10,1... | collective-permute-start | bytes 393224 | tf_op jit(solution)/shard_map/while/body/eval_jaxpr/ppermute | solution.py:14
  231.2 11.4 %collective-permute-start.1 = (bf16[2,256,128]{2,1,0:T(8,128)(2,1)S(1)}, bf16[2,256,128]{2,1,0:T(8,128)(2,1)S(1)}, u32[]{:S(2)}, u32[]{:S(2)}) collective-permute-start(bf16[2,256,128]{2,1,0:T(8,128)(2,1)S(1)} %copy.78), channel_id=1, source_target_pairs={{0,1},{1,2},{2,3},{3,4},{4,5},{5,6},{6,7},{7,8},{8,9},{9,10},{10,1... | collective-permute-start | bytes 393224 | tf_op jit(solution)/shard_map/while/body/eval_jaxpr/ppermute | solution.py:14
  245.3 11.4 %collective-permute-start.1 = (bf16[2,256,128]{2,1,0:T(8,128)(2,1)S(1)}, bf16[2,256,128]{2,1,0:T(8,128)(2,1)S(1)}, u32[]{:S(2)}, u32[]{:S(2)}) collective-permute-start(bf16[2,256,128]{2,1,0:T(8,128)(2,1)S(1)} %copy.78), channel_id=1, source_target_pairs={{0,1},{1,2},{2,3},{3,4},{4,5},{5,6},{6,7},{7,8},{8,9},{9,10},{10,1... | collective-permute-start | bytes 393224 | tf_op jit(solution)/shard_map/while/body/eval_jaxpr/ppermute | solution.py:14
  259.4 12.4 %collective-permute-start.1 = (bf16[2,256,128]{2,1,0:T(8,128)(2,1)S(1)}, bf16[2,256,128]{2,1,0:T(8,128)(2,1)S(1)}, u32[]{:S(2)}, u32[]{:S(2)}) collective-permute-start(bf16[2,256,128]{2,1,0:T(8,128)(2,1)S(1)} %copy.78), channel_id=1, source_target_pairs={{0,1},{1,2},{2,3},{3,4},{4,5},{5,6},{6,7},{7,8},{8,9},{9,10},{10,1... | collective-permute-start | bytes 393224 | tf_op jit(solution)/shard_map/while/body/eval_jaxpr/ppermute | solution.py:14
  274.4 10.8 %collective-permute-start.2 = (f32[2,256,128]{2,1,0:T(8,128)S(1)}, f32[2,256,128]{2,1,0:T(8,128)S(1)}, u32[]{:S(2)}, u32[]{:S(2)}) collective-permute-start(f32[2,256,128]{2,1,0:T(8,128)S(1)} %get-tuple-element.1137), channel_id=1, source_target_pairs={{15,0},{0,1},{1,2},{2,3},{3,4},{4,5},{5,6},{6,7},{7,8},{8,9},{9,10... | collective-permute-start | bytes 786440 | tf_op jit(solution)/shard_map/while/body/eval_jaxpr/ppermute | solution.py:20
  274.5 13.5 %collective-permute-start.1 = (bf16[2,256,128]{2,1,0:T(8,128)(2,1)S(1)}, bf16[2,256,128]{2,1,0:T(8,128)(2,1)S(1)}, u32[]{:S(2)}, u32[]{:S(2)}) collective-permute-start(bf16[2,256,128]{2,1,0:T(8,128)(2,1)S(1)} %copy.78), channel_id=1, source_target_pairs={{0,1},{1,2},{2,3},{3,4},{4,5},{5,6},{6,7},{7,8},{8,9},{9,10},{10,1... | collective-permute-start | bytes 393224 | tf_op jit(solution)/shard_map/while/body/eval_jaxpr/ppermute | solution.py:14
  290.6 11.9 %collective-permute-start.2 = (f32[2,256,128]{2,1,0:T(8,128)S(1)}, f32[2,256,128]{2,1,0:T(8,128)S(1)}, u32[]{:S(2)}, u32[]{:S(2)}) collective-permute-start(f32[2,256,128]{2,1,0:T(8,128)S(1)} %get-tuple-element.1137), channel_id=1, source_target_pairs={{15,0},{0,1},{1,2},{2,3},{3,4},{4,5},{5,6},{6,7},{7,8},{8,9},{9,10... | collective-permute-start | bytes 786440 | tf_op jit(solution)/shard_map/while/body/eval_jaxpr/ppermute | solution.py:20
  290.7 14.6 %collective-permute-start.1 = (bf16[2,256,128]{2,1,0:T(8,128)(2,1)S(1)}, bf16[2,256,128]{2,1,0:T(8,128)(2,1)S(1)}, u32[]{:S(2)}, u32[]{:S(2)}) collective-permute-start(bf16[2,256,128]{2,1,0:T(8,128)(2,1)S(1)} %copy.78), channel_id=1, source_target_pairs={{0,1},{1,2},{2,3},{3,4},{4,5},{5,6},{6,7},{7,8},{8,9},{9,10},{10,1... | collective-permute-start | bytes 393224 | tf_op jit(solution)/shard_map/while/body/eval_jaxpr/ppermute | solution.py:14
  307.9 12.9 %collective-permute-start.2 = (f32[2,256,128]{2,1,0:T(8,128)S(1)}, f32[2,256,128]{2,1,0:T(8,128)S(1)}, u32[]{:S(2)}, u32[]{:S(2)}) collective-permute-start(f32[2,256,128]{2,1,0:T(8,128)S(1)} %get-tuple-element.1137), channel_id=1, source_target_pairs={{15,0},{0,1},{1,2},{2,3},{3,4},{4,5},{5,6},{6,7},{7,8},{8,9},{9,10... | collective-permute-start | bytes 786440 | tf_op jit(solution)/shard_map/while/body/eval_jaxpr/ppermute | solution.py:20
  308.0 15.4 %collective-permute-start.1 = (bf16[2,256,128]{2,1,0:T(8,128)(2,1)S(1)}, bf16[2,256,128]{2,1,0:T(8,128)(2,1)S(1)}, u32[]{:S(2)}, u32[]{:S(2)}) collective-permute-start(bf16[2,256,128]{2,1,0:T(8,128)(2,1)S(1)} %copy.78), channel_id=1, source_target_pairs={{0,1},{1,2},{2,3},{3,4},{4,5},{5,6},{6,7},{7,8},{8,9},{9,10},{10,1... | collective-permute-start | bytes 393224 | tf_op jit(solution)/shard_map/while/body/eval_jaxpr/ppermute | solution.py:14
  326.1 12.9 %collective-permute-start.2 = (f32[2,256,128]{2,1,0:T(8,128)S(1)}, f32[2,256,128]{2,1,0:T(8,128)S(1)}, u32[]{:S(2)}, u32[]{:S(2)}) collective-permute-start(f32[2,256,128]{2,1,0:T(8,128)S(1)} %get-tuple-element.1137), channel_id=1, source_target_pairs={{15,0},{0,1},{1,2},{2,3},{3,4},{4,5},{5,6},{6,7},{7,8},{8,9},{9,10... | collective-permute-start | bytes 786440 | tf_op jit(solution)/shard_map/while/body/eval_jaxpr/ppermute | solution.py:20
  326.1 14.5 %collective-permute-start.1 = (bf16[2,256,128]{2,1,0:T(8,128)(2,1)S(1)}, bf16[2,256,128]{2,1,0:T(8,128)(2,1)S(1)}, u32[]{:S(2)}, u32[]{:S(2)}) collective-permute-start(bf16[2,256,128]{2,1,0:T(8,128)(2,1)S(1)} %copy.78), channel_id=1, source_target_pairs={{0,1},{1,2},{2,3},{3,4},{4,5},{5,6},{6,7},{7,8},{8,9},{9,10},{10,1... | collective-permute-start | bytes 393224 | tf_op jit(solution)/shard_map/while/body/eval_jaxpr/ppermute | solution.py:14
  343.3 12.4 %collective-permute-start.2 = (f32[2,256,128]{2,1,0:T(8,128)S(1)}, f32[2,256,128]{2,1,0:T(8,128)S(1)}, u32[]{:S(2)}, u32[]{:S(2)}) collective-permute-start(f32[2,256,128]{2,1,0:T(8,128)S(1)} %get-tuple-element.1137), channel_id=1, source_target_pairs={{15,0},{0,1},{1,2},{2,3},{3,4},{4,5},{5,6},{6,7},{7,8},{8,9},{9,10... | collective-permute-start | bytes 786440 | tf_op jit(solution)/shard_map/while/body/eval_jaxpr/ppermute | solution.py:20
  343.4 13.7 %collective-permute-start.1 = (bf16[2,256,128]{2,1,0:T(8,128)(2,1)S(1)}, bf16[2,256,128]{2,1,0:T(8,128)(2,1)S(1)}, u32[]{:S(2)}, u32[]{:S(2)}) collective-permute-start(bf16[2,256,128]{2,1,0:T(8,128)(2,1)S(1)} %copy.78), channel_id=1, source_target_pairs={{0,1},{1,2},{2,3},{3,4},{4,5},{5,6},{6,7},{7,8},{8,9},{9,10},{10,1... | collective-permute-start | bytes 393224 | tf_op jit(solution)/shard_map/while/body/eval_jaxpr/ppermute | solution.py:14
  359.7 11.4 %collective-permute-start.2 = (f32[2,256,128]{2,1,0:T(8,128)S(1)}, f32[2,256,128]{2,1,0:T(8,128)S(1)}, u32[]{:S(2)}, u32[]{:S(2)}) collective-permute-start(f32[2,256,128]{2,1,0:T(8,128)S(1)} %get-tuple-element.1137), channel_id=1, source_target_pairs={{15,0},{0,1},{1,2},{2,3},{3,4},{4,5},{5,6},{6,7},{7,8},{8,9},{9,10... | collective-permute-start | bytes 786440 | tf_op jit(solution)/shard_map/while/body/eval_jaxpr/ppermute | solution.py:20
  359.8 12.8 %collective-permute-start.1 = (bf16[2,256,128]{2,1,0:T(8,128)(2,1)S(1)}, bf16[2,256,128]{2,1,0:T(8,128)(2,1)S(1)}, u32[]{:S(2)}, u32[]{:S(2)}) collective-permute-start(bf16[2,256,128]{2,1,0:T(8,128)(2,1)S(1)} %copy.78), channel_id=1, source_target_pairs={{0,1},{1,2},{2,3},{3,4},{4,5},{5,6},{6,7},{7,8},{8,9},{9,10},{10,1... | collective-permute-start | bytes 393224 | tf_op jit(solution)/shard_map/while/body/eval_jaxpr/ppermute | solution.py:14
  375.2 10.5 %collective-permute-start.2 = (f32[2,256,128]{2,1,0:T(8,128)S(1)}, f32[2,256,128]{2,1,0:T(8,128)S(1)}, u32[]{:S(2)}, u32[]{:S(2)}) collective-permute-start(f32[2,256,128]{2,1,0:T(8,128)S(1)} %get-tuple-element.1137), channel_id=1, source_target_pairs={{15,0},{0,1},{1,2},{2,3},{3,4},{4,5},{5,6},{6,7},{7,8},{8,9},{9,10... | collective-permute-start | bytes 786440 | tf_op jit(solution)/shard_map/while/body/eval_jaxpr/ppermute | solution.py:20
  375.3 11.8 %collective-permute-start.1 = (bf16[2,256,128]{2,1,0:T(8,128)(2,1)S(1)}, bf16[2,256,128]{2,1,0:T(8,128)(2,1)S(1)}, u32[]{:S(2)}, u32[]{:S(2)}) collective-permute-start(bf16[2,256,128]{2,1,0:T(8,128)(2,1)S(1)} %copy.78), channel_id=1, source_target_pairs={{0,1},{1,2},{2,3},{3,4},{4,5},{5,6},{6,7},{7,8},{8,9},{9,10},{10,1... | collective-permute-start | bytes 393224 | tf_op jit(solution)/shard_map/while/body/eval_jaxpr/ppermute | solution.py:14
  389.8 11.4 %collective-permute-start.1 = (bf16[2,256,128]{2,1,0:T(8,128)(2,1)S(1)}, bf16[2,256,128]{2,1,0:T(8,128)(2,1)S(1)}, u32[]{:S(2)}, u32[]{:S(2)}) collective-permute-start(bf16[2,256,128]{2,1,0:T(8,128)(2,1)S(1)} %copy.78), channel_id=1, source_target_pairs={{0,1},{1,2},{2,3},{3,4},{4,5},{5,6},{6,7},{7,8},{8,9},{9,10},{10,1... | collective-permute-start | bytes 393224 | tf_op jit(solution)/shard_map/while/body/eval_jaxpr/ppermute | solution.py:14
  403.9 11.4 %collective-permute-start.1 = (bf16[2,256,128]{2,1,0:T(8,128)(2,1)S(1)}, bf16[2,256,128]{2,1,0:T(8,128)(2,1)S(1)}, u32[]{:S(2)}, u32[]{:S(2)}) collective-permute-start(bf16[2,256,128]{2,1,0:T(8,128)(2,1)S(1)} %copy.78), channel_id=1, source_target_pairs={{0,1},{1,2},{2,3},{3,4},{4,5},{5,6},{6,7},{7,8},{8,9},{9,10},{10,1... | collective-permute-start | bytes 393224 | tf_op jit(solution)/shard_map/while/body/eval_jaxpr/ppermute | solution.py:14
  418.0 11.4 %collective-permute-start.1 = (bf16[2,256,128]{2,1,0:T(8,128)(2,1)S(1)}, bf16[2,256,128]{2,1,0:T(8,128)(2,1)S(1)}, u32[]{:S(2)}, u32[]{:S(2)}) collective-permute-start(bf16[2,256,128]{2,1,0:T(8,128)(2,1)S(1)} %copy.78), channel_id=1, source_target_pairs={{0,1},{1,2},{2,3},{3,4},{4,5},{5,6},{6,7},{7,8},{8,9},{9,10},{10,1... | collective-permute-start | bytes 393224 | tf_op jit(solution)/shard_map/while/body/eval_jaxpr/ppermute | solution.py:14
  (18 other events, 170.6 us)
where the time goes:
time: 433 us; the launch traced here: 431 us
  waiting for transfers between devices  265 us (61%)
  starting transfers between devices  62.8 us (15%)
  local copies, waits for them, and re-layouts  41.6 us (10%)
  loops' own time  41.3 us (10%)
  other arithmetic  9.99 us (2%)
  matrix products  8.17 us (2%)
    ppermute x16, waiting for transfers between devices, passed_along(): return lax.ppermute(block, axis, route)  144 us
    ppermute x31, waiting for transfers between devices, shifted(): return lax.ppermute(value, axis, pairs)  121 us
    ppermute x31, starting transfers between devices, shifted(): return lax.ppermute(value, axis, pairs)  61.4 us
    another operation x1, loops' own time, shards(): lax.fori_loop(0, cycle_size, bwd_travel, (kv_pair, zeros_kv, zeros_query))  21.3 us
    another operation x1, loops' own time, shards(): lax.fori_loop(1, cycle_size, fwd_travel, (kv_pair, first_stats))  19.5 us
    slice x31, local copies, waits for them, and re-layouts, pair_mask(): key_docs[key_count - 1] >= query_docs[0]  19 us
    slice x32, local copies, waits for them, and re-layouts, pair_mask(): query_docs[0]  17.6 us
  transfers between devices with their start and end apart: 47, of which 47 were waited for; matrix products, arithmetic and copies ran while one was open for 4% of the time, Pallas kernels for 0%

commit v1 on v0

v1 whole, which is shorter than its diff:
```python
import functools
import math

import jax
import jax.numpy as jnp
from jax import lax
from jax.experimental import pallas as pl
from jax.experimental.pallas import tpu as pltpu
from jax.sharding import PartitionSpec as P

MESH = pl.DeviceIdType.MESH
MASKED = -1e30
HEADS = 8
WIDTH = 128
ROWS = 256
REACH = 4
FIRST = 4
DOCS = 16


def attention_kernel(
    size,
    lengths,
    q_hbm,
    k_hbm,
    v_hbm,
    o_hbm,
    dq_out,
    dk_out,
    dv_out,
    q_ref,
    o_ref,
    keys,
    values,
    keys_turned,
    bias,
    weights,
    dots,
    tops,
    totals,
    weighted,
    factors,
    deltas,
    dq_acc,
    key_part,
    value_part,
    send_box,
    recv_box,
    load_sem,
    kv_send_sem,
    kv_recv_sem,
    grad_send_sem,
    grad_recv_sem,
):
    me = lax.axis_index("ctx")
    depth = jnp.where(me < FIRST, me, me - FIRST)
    has_left = depth > 0
    has_right = (me != FIRST - 1) & (me != size - 1)
    left = jnp.maximum(me - 1, 0)
    right = jnp.minimum(me + 1, size - 1)

    loads = [
        pltpu.make_async_copy(k_hbm, keys.at[0], load_sem.at[0]),
        pltpu.make_async_copy(v_hbm, values.at[0], load_sem.at[1]),
        pltpu.make_async_copy(q_hbm, q_ref, load_sem.at[2]),
        pltpu.make_async_copy(o_hbm, o_ref, load_sem.at[3]),
    ]
    for load in loads:
        load.start()

    barrier = pltpu.get_barrier_semaphore()

    @pl.when(has_left)
    def _():
        pl.semaphore_signal(barrier, inc=1, device_id={"ctx": left}, device_id_type=MESH)

    @pl.when(has_right)
    def _():
        pl.semaphore_signal(barrier, inc=1, device_id={"ctx": right}, device_id_type=MESH)

    pl.semaphore_wait(barrier, has_left.astype(jnp.int32) + has_right.astype(jnp.int32))

    def forward(k, part):
        place = (keys, values)[part]
        source = (k_hbm, v_hbm)[part] if k == 0 else place.at[k]
        return pltpu.make_async_remote_copy(
            src_ref=source,
            dst_ref=place.at[k + 1],
            send_sem=kv_send_sem.at[k, part],
            recv_sem=kv_recv_sem.at[k + 1, part],
            device_id={"ctx": right},
            device_id_type=MESH,
        )

    def send_forward(k, part):
        @pl.when(has_right & (depth >= k))
        def _():
            forward(k, part).start()

    send_forward(0, 0)
    send_forward(0, 1)

    places = me * ROWS + lax.broadcasted_iota(jnp.int32, (8, ROWS), 1)
    starts = jnp.zeros((8, ROWS), jnp.int32)
    end = jnp.int32(0)
    for d in range(DOCS):
        end = end + lengths[d]
        starts = jnp.where(places >= end, end, starts)
    places, starts = places[:1], starts[:1]

    def make_bias(k):
        key_places = (me - k) * ROWS + lax.broadcasted_iota(jnp.int32, (ROWS, ROWS), 0)
        allowed = (key_places >= starts) & (key_places <= places)
        bias[k] = jnp.where(allowed, 0.0, MASKED)

    to_log2 = math.log2(math.e) / math.sqrt(WIDTH)
    score_scale = 1.0 / math.sqrt(WIDTH)
    tops[...] = jnp.full(tops.shape, MASKED, jnp.float32)
    totals[...] = jnp.zeros(totals.shape, jnp.float32)
    weighted[...] = jnp.zeros(weighted.shape, jnp.float32)
    for k in range(REACH + 1):
        make_bias(k)

    def head(ref, h):
        return ref[:, h * WIDTH : (h + 1) * WIDTH]

    def scores(k):
        block = keys[k]
        for h in range(HEADS):
            raw = lax.dot_general(
                block, head(q_ref, h), (((1,), (1,)), ((), ())), preferred_element_type=jnp.float32
            )
            raw = raw * to_log2 + bias[k]
            top = jnp.max(raw, axis=0, keepdims=True)
            grown = jnp.exp2(raw - top)
            tops[k, h : h + 1, :] = top
            totals[k, h : h + 1, :] = jnp.sum(grown, axis=0, keepdims=True)
            weights[k, h] = grown
        keys_turned[k] = block.T

    def grad_dots(k):
        block = values[k]
        for h in range(HEADS):
            dot = lax.dot_general(
                block, head(o_ref, h), (((1,), (1,)), ((), ())), preferred_element_type=jnp.float32
            )
            dots[k, h] = dot
            weighted[k, h : h + 1, :] = jnp.sum(weights[k, h] * dot, axis=0, keepdims=True)

    loads[0].wait()
    loads[2].wait()
    scores(0)
    loads[1].wait()
    loads[3].wait()
    grad_dots(0)

    for k in range(1, REACH + 1):

        @pl.when(depth >= k)
        def _(k=k):
            forward(k - 1, 0).wait_recv()
            if k < REACH:
                send_forward(k, 0)
            scores(k)
            forward(k - 1, 1).wait_recv()
            if k < REACH:
                send_forward(k, 1)
            grad_dots(k)

    top = tops[0]
    for k in range(1, REACH + 1):
        top = jnp.maximum(top, tops[k])
    total = jnp.zeros_like(top)
    weight = jnp.zeros_like(top)
    for k in range(REACH + 1):
        factor = jnp.exp2(tops[k] - top)
        factors[k] = factor
        total = total + factor * totals[k]
        weight = weight + factor * weighted[k]
    inverse = 1.0 / total
    deltas[...] = weight * inverse
    for k in range(REACH + 1):
        factors[k] = factors[k] * inverse
    dq_acc[...] = jnp.zeros(dq_acc.shape, jnp.float32)

    def send_back(k, part):
        return pltpu.make_async_remote_copy(
            src_ref=send_box.at[k, part],
            dst_ref=recv_box.at[k - 1, part],
            send_sem=grad_send_sem.at[k, part],
            recv_sem=grad_recv_sem.at[k - 1, part],
            device_id={"ctx": left},
            device_id_type=MESH,
        )

    def gradients(k):
        key_sum = jnp.zeros((ROWS, WIDTH), jnp.float32)
        value_sum = jnp.zeros((ROWS, WIDTH), jnp.float32)
        for h in range(HEADS):
            soft = weights[k, h] * factors[k, h : h + 1, :]
            score_grad = soft * (dots[k, h] - deltas[h : h + 1, :])
            soft_low = soft.astype(jnp.bfloat16)
            grad_low = score_grad.astype(jnp.bfloat16)
            value_sum = value_sum + jnp.dot(soft_low, head(o_ref, h), preferred_element_type=jnp.float32)
            key_sum = key_sum + jnp.dot(grad_low, head(q_ref, h), preferred_element_type=jnp.float32)
            dq_acc[h] += jnp.dot(keys_turned[k], grad_low, preferred_element_type=jnp.float32)
        value_part[...] = value_sum
        key_part[...] = key_sum

    for k in range(REACH, -1, -1):

        @pl.when(depth >= k)
        def _(k=k):
            gradients(k)
            for part, own in ((0, value_part), (1, key_part)):
                if k < REACH:

                    @pl.when(has_right)
                    def _():
                        send_back(k + 1, part).wait_recv()
                        own[...] += recv_box[k, part].astype(jnp.float32)

                if k > 0:
                    send_box[k, part] = own[...].astype(jnp.bfloat16)
                    send_back(k, part).start()
                elif part == 0:
                    dv_out[...] = own[...].astype(jnp.bfloat16)
                else:
                    dk_out[...] = (own[...] * score_scale).astype(jnp.bfloat16)

    for h in range(HEADS):
        dq_out[:, h * WIDTH : (h + 1) * WIDTH] = (dq_acc[h] * score_scale).T.astype(jnp.bfloat16)

    for k in range(REACH):

        @pl.when(has_right & (depth >= k))
        def _(k=k):
            forward(k, 0).wait_send()
            forward(k, 1).wait_send()

    for k in range(1, REACH + 1):

        @pl.when(depth >= k)
        def _(k=k):
            send_back(k, 0).wait_send()
            send_back(k, 1).wait_send()


def shards(size, query_rows, key_rows, value_rows, out_grad, doc_lengths):
    bf16, f32 = jnp.bfloat16, jnp.float32
    blocks = REACH + 1
    in_place = pl.BlockSpec(memory_space=pl.ANY)
    in_vmem = pl.BlockSpec(memory_space=pltpu.VMEM)
    return pl.pallas_call(
        functools.partial(attention_kernel, size),
        out_shape=(
            jax.ShapeDtypeStruct(query_rows.shape, bf16),
            jax.ShapeDtypeStruct(key_rows.shape, bf16),
            jax.ShapeDtypeStruct(value_rows.shape, bf16),
        ),
        in_specs=[pl.BlockSpec(memory_space=pltpu.SMEM)] + [in_place] * 4,
        out_specs=(in_vmem, in_vmem, in_vmem),
        scratch_shapes=[
            pltpu.VMEM((ROWS, HEADS * WIDTH), bf16),
            pltpu.VMEM((ROWS, HEADS * WIDTH), bf16),
            pltpu.VMEM((blocks, ROWS, WIDTH), bf16),
            pltpu.VMEM((blocks, ROWS, WIDTH), bf16),
            pltpu.VMEM((blocks, WIDTH, ROWS), bf16),
            pltpu.VMEM((blocks, ROWS, ROWS), f32),
            pltpu.VMEM((blocks, HEADS, ROWS, ROWS), f32),
            pltpu.VMEM((blocks, HEADS, ROWS, ROWS), f32),
            pltpu.VMEM((blocks, HEADS, ROWS), f32),
            pltpu.VMEM((blocks, HEADS, ROWS), f32),
            pltpu.VMEM((blocks, HEADS, ROWS), f32),
            pltpu.VMEM((blocks, HEADS, ROWS), f32),
            pltpu.VMEM((HEADS, ROWS), f32),
            pltpu.VMEM((HEADS, WIDTH, ROWS), f32),
            pltpu.VMEM((ROWS, WIDTH), f32),
            pltpu.VMEM((ROWS, WIDTH), f32),
            pltpu.VMEM((blocks, 2, ROWS, WIDTH), bf16),
            pltpu.VMEM((blocks, 2, ROWS, WIDTH), bf16),
            pltpu.SemaphoreType.DMA((4,)),
            pltpu.SemaphoreType.DMA((blocks, 2)),
            pltpu.SemaphoreType.DMA((blocks, 2)),
            pltpu.SemaphoreType.DMA((blocks, 2)),
            pltpu.SemaphoreType.DMA((blocks, 2)),
        ],
        compiler_params=pltpu.CompilerParams(
            collective_id=0, has_side_effects=True, vmem_limit_bytes=48 * 1024 * 1024
        ),
    )(doc_lengths, query_rows, key_rows, value_rows, out_grad)


def solution(mesh):
    rows = P(("dp", "ctx"), None)
    return jax.shard_map(
        functools.partial(shards, mesh.shape["ctx"]),
        mesh=mesh,
        in_specs=(rows, rows, rows, rows, P("dp")),
        out_specs=(rows, rows, rows),
        check_vma=False,
    )
```

time: 433 us -> 48.4 us (0.11)
  waiting for transfers between devices: 265 us -> 0 us
  starting transfers between devices: 62.8 us -> 0 us
  loops' own time: 41.3 us -> 0 us
  Pallas kernels: 0 us -> 41 us
  local copies, waits for them, and re-layouts: 41.6 us -> 6.46 us
  other arithmetic: 9.99 us -> 0 us
  matrix products: 8.17 us -> 0 us
    ppermute x47 -> x0, waiting for transfers between devices: 265 us -> none  [the longest x16 144 us: passed_along(): return lax.ppermute(block, axis, route)]
    ppermute x47 -> x0, starting transfers between devices: 62.8 us -> none  [the longest x31 61.4 us: shifted(): return lax.ppermute(value, axis, pairs)]
    another operation x34 -> x0, loops' own time: 41.3 us -> none  [the longest x1 21.3 us: shards(): lax.fori_loop(0, cycle_size, bwd_travel, (kv_pair, zeros_kv, zeros_query))]
    pallas_call x0 -> x1, Pallas kernels: none -> 41 us  [shards(): pl.pallas_call(functools.partial(attention_kernel, size), out_shape=(jax....]
    slice x63 -> x0, local copies, waits for them, and re-layouts: 36.6 us -> none  [the longest x31 19 us: pair_mask(): key_docs[key_count - 1] >= query_docs[0]]
    dot_general x14 -> x0, matrix products: 8.17 us -> none  [the longest x4 3.17 us: scores_of(): jnp.einsum('thd,sd->ths', grads_out, kv_block[1], preferred_element_type=...]
    reduce_sum x34 -> x0, other arithmetic: 4.51 us -> none  [the longest x32 2.78 us: doc_numbers(): jnp.sum((positions[:, None] >= doc_ends[None, :]).astype(jnp.int32), axis=1)]
    unnamed x11 -> x13, local copies, waits for them, and re-layouts: 2.02 us -> 6.46 us
  transfers between devices with their start and end apart: 47 -> 0, of which waited for: 47 -> 0; matrix products, arithmetic and copies ran while one was open for 4% -> 0% of each run, Pallas kernels for 0% -> 0%
where the time goes in v1:
time: 48.4 us; the launch traced here: 48.1 us
  Pallas kernels  41 us (85%)
  local copies, waits for them, and re-layouts  6.46 us (13%)
  between operations  0.65 us (1%)
    pallas_call x1, Pallas kernels, shards(): pl.pallas_call(functools.partial(attention_kernel, size), out_shape=(jax....  41 us
    unnamed x13, local copies, waits for them, and re-layouts  6.46 us

profile of v1, /device:TPU:22, one launch (start us, length us, event | category | flops | bytes accessed | tf_op | source)
XLA Modules:
  0.0 48.1 jit_solution(16167027175704278129)
XLA Ops:
  0.6 0.0 copy-start
  0.6 1.0 %copy-done = bf16[256,1024]{1,0:T(8,128)(2,1)S(1)} copy-done((bf16[256,1024]{1,0:T(8,128)(2,1)S(1)}, bf16[256,1024]{1,0:T(8,128)(2,1)}, u32[]{:S(2)}) %copy-start) | copy-done | bytes 524312
  1.7 0.0 copy-start.1
  1.7 1.0 %copy-done.1 = bf16[256,1024]{1,0:T(8,128)(2,1)S(1)} copy-done((bf16[256,1024]{1,0:T(8,128)(2,1)S(1)}, bf16[256,1024]{1,0:T(8,128)(2,1)}, u32[]{:S(2)}) %copy-start.1) | copy-done | bytes 524312
  2.7 0.0 copy-start.2
  2.7 0.8 %copy-done.2 = bf16[256,128]{1,0:T(8,128)(2,1)S(1)} copy-done((bf16[256,128]{1,0:T(8,128)(2,1)S(1)}, bf16[256,128]{1,0:T(8,128)(2,1)}, u32[]{:S(2)}) %copy-start.2) | copy-done | bytes 65560
  3.6 0.0 copy-start.3
  3.6 0.8 %copy-done.3 = bf16[256,128]{1,0:T(8,128)(2,1)S(1)} copy-done((bf16[256,128]{1,0:T(8,128)(2,1)S(1)}, bf16[256,128]{1,0:T(8,128)(2,1)}, u32[]{:S(2)}) %copy-start.3) | copy-done | bytes 65560
  4.4 0.0 copy-start.4
  4.4 0.7 %copy-done.4 = s32[16]{0:T(128)S(1)} copy-done((s32[16]{0:T(128)S(1)}, s32[16]{0:T(128)}, u32[]{:S(2)}) %copy-start.4) | copy-done | bytes 88
  5.1 41.0 %shard_map.76 = (bf16[256,1024]{1,0:T(8,128)(2,1)S(1)}, bf16[256,128]{1,0:T(8,128)(2,1)S(1)}, bf16[256,128]{1,0:T(8,128)(2,1)S(1)}) custom-call(s32[16]{0:T(128)S(1)} %copy-done.4, bf16[256,1024]{1,0:T(8,128)(2,1)S(1)} %copy-done, bf16[256,128]{1,0:T(8,128)(2,1)S(1)} %copy-done.2, bf16[256,128]{1,0:T(8,128)(2,1)S(1)} %copy-done.3, ...), custom_call_target="tpu_custom_call" | custom-call | tf_op jit(solution)/shard_map/pallas_call | solution.py:254
  46.1 0.8 %copy.11 = bf16[256,1024]{1,0:T(8,128)(2,1)} copy(bf16[256,1024]{1,0:T(8,128)(2,1)S(1)} %get-tuple-element.6) | data formatting | bytes 1048576
  46.9 0.6 %copy.12 = bf16[256,128]{1,0:T(8,128)(2,1)} copy(bf16[256,128]{1,0:T(8,128)(2,1)S(1)} %get-tuple-element.7) | data formatting | bytes 131072
  47.5 0.6 %copy.13 = bf16[256,128]{1,0:T(8,128)(2,1)} copy(bf16[256,128]{1,0:T(8,128)(2,1)S(1)} %get-tuple-element.8) | data formatting | bytes 131072
Async XLA Ops:
  0.6 1.0 %copy-start = (bf16[256,1024]{1,0:T(8,128)(2,1)S(1)}, bf16[256,1024]{1,0:T(8,128)(2,1)}, u32[]{:S(2)}) copy-start(bf16[256,1024]{1,0:T(8,128)(2,1)} %q_hbm.1) | copy-start | bytes 1572868
  1.7 1.0 %copy-start.1 = (bf16[256,1024]{1,0:T(8,128)(2,1)S(1)}, bf16[256,1024]{1,0:T(8,128)(2,1)}, u32[]{:S(2)}) copy-start(bf16[256,1024]{1,0:T(8,128)(2,1)} %o_hbm.1) | copy-start | bytes 1572868
  2.7 0.8 %copy-start.2 = (bf16[256,128]{1,0:T(8,128)(2,1)S(1)}, bf16[256,128]{1,0:T(8,128)(2,1)}, u32[]{:S(2)}) copy-start(bf16[256,128]{1,0:T(8,128)(2,1)} %k_hbm.1) | copy-start | bytes 196612
  3.6 0.8 %copy-start.3 = (bf16[256,128]{1,0:T(8,128)(2,1)S(1)}, bf16[256,128]{1,0:T(8,128)(2,1)}, u32[]{:S(2)}) copy-start(bf16[256,128]{1,0:T(8,128)(2,1)} %v_hbm.1) | copy-start | bytes 196612
  4.4 0.7 %copy-start.4 = (s32[16]{0:T(128)S(1)}, s32[16]{0:T(128)}, u32[]{:S(2)}) copy-start(s32[16]{0:T(128)} %lengths.1) | copy-start | bytes 196

commit v2 on v1

v2 whole, which is shorter than its diff:
```python
import functools
import math

import jax
import jax.numpy as jnp
from jax import lax
from jax.experimental import pallas as pl
from jax.experimental.pallas import tpu as pltpu
from jax.sharding import PartitionSpec as P

MESH = pl.DeviceIdType.MESH
MASKED = -1e30
HEADS = 8
WIDTH = 128
ROWS = 256
HALF = ROWS // 2
REACH = 4
FIRST = 4
DOCS = 16
CHUNKS = 4


def attention_kernel(
    lengths_hbm,
    q_hbm,
    k_hbm,
    v_hbm,
    o_hbm,
    dq_out,
    dk_out,
    dv_out,
    lengths,
    q_ref,
    o_ref,
    keys,
    values,
    passing,
    keys_turned,
    bias,
    weights,
    dots,
    tops,
    totals,
    weighted,
    factors,
    deltas,
    dq_acc,
    key_part,
    value_part,
    send_box,
    recv_box,
    far_box,
    passing_back,
    load_sem,
    kv_send_sem,
    kv_recv_sem,
    grad_send_sem,
    grad_recv_sem,
    far_send_sem,
    far_recv_sem,
):
    me = lax.axis_index("ctx")
    size = 16
    depth = jnp.where(me < FIRST, me, me - FIRST)
    has_left = depth > 0
    has_right = (me != FIRST - 1) & (me != size - 1)
    left = jnp.maximum(me - 1, 0)
    right = jnp.minimum(me + 1, size - 1)

    out_far = (me >= 4) & (me < 12)
    out_relay = jnp.where(me < 6, me - 2, jnp.where(me < 10, me + 6, me - 10))
    is_relay = (me < 4) | (me >= 12)
    relay_from = jnp.where(me < 2, me + 10, jnp.where(me < 4, me + 2, me - 6))
    relay_to = jnp.where(me < 2, me + 14, jnp.where(me < 4, me + 6, me - 2))
    in_far = me >= 8
    in_relay = jnp.where(me < 10, me - 6, jnp.where(me < 14, me + 2, me - 14))
    back_far = me >= 8
    back_relay = jnp.where(me < 14, me - 6, me - 14)
    is_back_relay = me < 8
    back_relay_from = jnp.where(me < 2, me + 14, me + 6)
    back_relay_to = jnp.where(me < 2, me + 10, me + 2)
    in_back = (me >= 4) & (me < 12)
    in_back_relay = jnp.where(me < 10, me - 2, me - 10)

    loads = [
        pltpu.make_async_copy(lengths_hbm, lengths, load_sem.at[4]),
        pltpu.make_async_copy(k_hbm, keys.at[0], load_sem.at[0]),
        pltpu.make_async_copy(v_hbm, values.at[0], load_sem.at[1]),
        pltpu.make_async_copy(q_hbm, q_ref, load_sem.at[2]),
        pltpu.make_async_copy(o_hbm, o_ref, load_sem.at[3]),
    ]
    for load in loads:
        load.start()

    barrier = pltpu.get_barrier_semaphore()

    def greet(condition, device):
        @pl.when(condition)
        def _():
            pl.semaphore_signal(barrier, inc=1, device_id={"ctx": device}, device_id_type=MESH)

    greet(has_left, left)
    greet(has_right, right)
    greet(is_relay, relay_from)
    greet(in_far, in_relay)
    greet(is_back_relay, back_relay_from)
    greet(in_back, in_back_relay)
    targets = (has_left, has_right, out_far, is_relay, back_far, is_back_relay)
    pl.semaphore_wait(barrier, sum(target.astype(jnp.int32) for target in targets))

    def remote(source, target, send, recv, device):
        return pltpu.make_async_remote_copy(
            src_ref=source, dst_ref=target, send_sem=send, recv_sem=recv, device_id={"ctx": device}, device_id_type=MESH
        )

    def piece(c):
        return c // 2, pl.ds((c % 2) * HALF, HALF)

    def own_piece(c):
        part, rows = piece(c)
        return (k_hbm, v_hbm)[part].at[rows]

    def forward(k, c):
        part, rows = piece(c)
        place = (keys, values)[part]
        source = own_piece(c) if k == 0 else place.at[k, rows]
        return remote(source, place.at[k + 1, rows], kv_send_sem.at[k, c], kv_recv_sem.at[k + 1, c], right)

    def to_relay(c):
        part, rows = piece(c)
        return remote(own_piece(c), passing.at[part, rows], far_send_sem.at[0, c], far_recv_sem.at[0, c], out_relay)

    def from_relay(c):
        part, rows = piece(c)
        target = (keys, values)[part].at[REACH, rows]
        return remote(passing.at[part, rows], target, far_send_sem.at[1, c], far_recv_sem.at[1, c], relay_to)

    def send_forward(k, c):
        @pl.when(has_right & (depth >= k))
        def _():
            forward(k, c).start()

    def relay(c):
        @pl.when(is_relay)
        def _():
            to_relay(c).wait_recv()
            from_relay(c).start()

    for c in range(CHUNKS):
        send_forward(0, c)

        @pl.when(out_far)
        def _(c=c):
            to_relay(c).start()

    loads[0].wait()
    places = me * ROWS + lax.broadcasted_iota(jnp.int32, (8, ROWS), 1)
    starts = jnp.zeros((8, ROWS), jnp.int32)
    end = jnp.int32(0)
    for d in range(DOCS):
        end = end + lengths[d]
        starts = jnp.where(places >= end, end, starts)
    places, starts = places[:1], starts[:1]
    for k in range(REACH + 1):
        key_places = (me - k) * ROWS + lax.broadcasted_iota(jnp.int32, (ROWS, ROWS), 0)
        allowed = (key_places >= starts) & (key_places <= places)
        bias[k] = jnp.where(allowed, 0.0, MASKED)

    to_log2 = math.log2(math.e) / math.sqrt(WIDTH)
    score_scale = 1.0 / math.sqrt(WIDTH)
    tops[...] = jnp.full(tops.shape, MASKED, jnp.float32)
    totals[...] = jnp.zeros(totals.shape, jnp.float32)
    weighted[...] = jnp.zeros(weighted.shape, jnp.float32)

    def head(ref, h):
        return ref[:, h * WIDTH : (h + 1) * WIDTH]

    def scores(k):
        block = keys[k]
        for h in range(HEADS):
            raw = lax.dot_general(
                block, head(q_ref, h), (((1,), (1,)), ((), ())), preferred_element_type=jnp.float32
            )
            raw = raw * to_log2 + bias[k]
            top = jnp.max(raw, axis=0, keepdims=True)
            grown = jnp.exp2(raw - top)
            tops[k, h : h + 1, :] = top
            totals[k, h : h + 1, :] = jnp.sum(grown, axis=0, keepdims=True)
            weights[k, h] = grown
        keys_turned[k] = block.T

    def grad_dots(k):
        block = values[k]
        for h in range(HEADS):
            dot = lax.dot_general(
                block, head(o_ref, h), (((1,), (1,)), ((), ())), preferred_element_type=jnp.float32
            )
            dots[k, h] = dot
            weighted[k, h : h + 1, :] = jnp.sum(weights[k, h] * dot, axis=0, keepdims=True)

    def when_reached(k, *steps):
        @pl.when(depth >= k)
        def _():
            for step in steps:
                step()

    def arrive(k, c):
        def step():
            if k == REACH:
                from_relay(c).wait_recv()
            else:
                forward(k - 1, c).wait_recv()
                if k < REACH - 1:
                    send_forward(k, c)

        return step

    loads[1].wait()
    loads[3].wait()
    scores(0)
    loads[2].wait()
    loads[4].wait()
    grad_dots(0)

    when_reached(1, arrive(1, 0), arrive(1, 1))
    relay(0)
    when_reached(1, arrive(1, 2), arrive(1, 3))
    relay(1)
    when_reached(1, lambda: scores(1))
    when_reached(2, arrive(2, 0), arrive(2, 1))
    relay(2)
    when_reached(1, lambda: grad_dots(1))
    when_reached(2, arrive(2, 2), arrive(2, 3))
    relay(3)
    when_reached(2, lambda: scores(2))
    when_reached(3, arrive(3, 0), arrive(3, 1), lambda: grad_dots(2), lambda: scores(3))

    @pl.when(depth == 2)
    def _():
        grad_dots(2)

    when_reached(3, arrive(3, 2), arrive(3, 3), lambda: grad_dots(3))
    when_reached(4, arrive(4, 0), arrive(4, 1), lambda: scores(4), arrive(4, 2), arrive(4, 3), lambda: grad_dots(4))

    top = tops[0]
    for k in range(1, REACH + 1):
        top = jnp.maximum(top, tops[k])
    total = jnp.zeros_like(top)
    weight = jnp.zeros_like(top)
    for k in range(REACH + 1):
        factor = jnp.exp2(tops[k] - top)
        factors[k] = factor
        total = total + factor * totals[k]
        weight = weight + factor * weighted[k]
    inverse = 1.0 / total
    deltas[...] = weight * inverse
    for k in range(REACH + 1):
        factors[k] = factors[k] * inverse
    dq_acc[...] = jnp.zeros(dq_acc.shape, jnp.float32)

    def gradients(k):
        key_sum = jnp.zeros((ROWS, WIDTH), jnp.float32)
        value_sum = jnp.zeros((ROWS, WIDTH), jnp.float32)
        for h in range(HEADS):
            soft = weights[k, h] * factors[k, h : h + 1, :]
            score_grad = soft * (dots[k, h] - deltas[h : h + 1, :])
            soft_low = soft.astype(jnp.bfloat16)
            grad_low = score_grad.astype(jnp.bfloat16)
            value_sum = value_sum + jnp.dot(soft_low, head(o_ref, h), preferred_element_type=jnp.float32)
            key_sum = key_sum + jnp.dot(grad_low, head(q_ref, h), preferred_element_type=jnp.float32)
            dq_acc[h] += jnp.dot(keys_turned[k], grad_low, preferred_element_type=jnp.float32)
        value_part[...] = value_sum
        key_part[...] = key_sum

    own_parts = (value_part, key_part)

    def send_back(k, c):
        part, rows = piece(c)
        return remote(
            send_box.at[k, part, rows], recv_box.at[k - 1, part, rows], grad_send_sem.at[k, c], grad_recv_sem.at[k - 1, c], left
        )

    def back_to_relay(c):
        part, rows = piece(c)
        return remote(
            send_box.at[REACH, part, rows], passing_back.at[part, rows], far_send_sem.at[2, c], far_recv_sem.at[2, c], back_relay
        )

    def back_from_relay(c):
        part, rows = piece(c)
        return remote(
            passing_back.at[part, rows], far_box.at[part, rows], far_send_sem.at[3, c], far_recv_sem.at[3, c], back_relay_to
        )

    def relay_back(condition, chunks):
        @pl.when(condition)
        def _():
            for c in chunks:
                back_to_relay(c).wait_recv()
                back_from_relay(c).start()

    def pass_back(k):
        for c in range(CHUNKS):
            part, rows = piece(c)
            own = own_parts[part]
            if k < REACH - 1:

                @pl.when(has_right)
                def _(c=c, part=part, rows=rows, own=own):
                    send_back(k + 1, c).wait_recv()
                    own[rows] += recv_box[k, part, rows].astype(jnp.float32)

            send_box[k, part, rows] = own[rows].astype(jnp.bfloat16)
            (back_to_relay(c) if k == REACH else send_back(k, c)).start()

    for k in (3, 4, 2):
        when_reached(k, lambda k=k: gradients(k), lambda k=k: pass_back(k))
    relay_back((me >= 4) & (me < 8), (0, 1))
    when_reached(1, lambda: gradients(1), lambda: pass_back(1))
    relay_back((me >= 4) & (me < 8), (2, 3))
    gradients(0)
    for h in range(HEADS):
        dq_out[:, h * WIDTH : (h + 1) * WIDTH] = (dq_acc[h] * score_scale).T.astype(jnp.bfloat16)

    @pl.when(has_right)
    def _():
        for c in range(CHUNKS):
            part, rows = piece(c)
            send_back(1, c).wait_recv()
            own_parts[part][rows] += recv_box[0, part, rows].astype(jnp.float32)

    relay_back(me < 4, range(CHUNKS))

    @pl.when(in_back)
    def _():
        for c in range(CHUNKS):
            part, rows = piece(c)
            back_from_relay(c).wait_recv()
            own_parts[part][rows] += far_box[part, rows].astype(jnp.float32)

    dv_out[...] = value_part[...].astype(jnp.bfloat16)
    dk_out[...] = (key_part[...] * score_scale).astype(jnp.bfloat16)

    def sent(condition, copy):
        @pl.when(condition)
        def _():
            for c in range(CHUNKS):
                copy(c).wait_send()

    for k in range(REACH - 1):
        sent(has_right & (depth >= k), functools.partial(forward, k))
        sent(depth >= k + 1, functools.partial(send_back, k + 1))
    sent(out_far, to_relay)
    sent(is_relay, from_relay)
    sent(back_far, back_to_relay)
    sent(is_back_relay, back_from_relay)


def store_kernel(dq, dk, dv, dq_out, dk_out, dv_out, sem):
    copies = [
        pltpu.make_async_copy(dq, dq_out, sem.at[0]),
        pltpu.make_async_copy(dk, dk_out, sem.at[1]),
        pltpu.make_async_copy(dv, dv_out, sem.at[2]),
    ]
    for copy in copies:
        copy.start()
    for copy in copies:
        copy.wait()


def shards(query_rows, key_rows, value_rows, out_grad, doc_lengths):
    bf16, f32 = jnp.bfloat16, jnp.float32
    blocks = REACH + 1
    in_hbm = pl.BlockSpec(memory_space=pltpu.HBM)
    in_vmem = pl.BlockSpec(memory_space=pltpu.VMEM)
    operands = [
        pltpu.with_memory_space_constraint(array, pltpu.HBM)
        for array in (doc_lengths, query_rows, key_rows, value_rows, out_grad)
    ]
    results = tuple(jax.ShapeDtypeStruct(array.shape, bf16) for array in (query_rows, key_rows, value_rows))
    gradients = pl.pallas_call(
        attention_kernel,
        out_shape=results,
        in_specs=[in_hbm] * 5,
        out_specs=(in_vmem, in_vmem, in_vmem),
        scratch_shapes=[
            pltpu.SMEM((DOCS,), jnp.int32),
            pltpu.VMEM((ROWS, HEADS * WIDTH), bf16),
            pltpu.VMEM((ROWS, HEADS * WIDTH), bf16),
            pltpu.VMEM((blocks, ROWS, WIDTH), bf16),
            pltpu.VMEM((blocks, ROWS, WIDTH), bf16),
            pltpu.VMEM((2, ROWS, WIDTH), bf16),
            pltpu.VMEM((blocks, WIDTH, ROWS), bf16),
            pltpu.VMEM((blocks, ROWS, ROWS), f32),
            pltpu.VMEM((blocks, HEADS, ROWS, ROWS), f32),
            pltpu.VMEM((blocks, HEADS, ROWS, ROWS), f32),
            pltpu.VMEM((blocks, HEADS, ROWS), f32),
            pltpu.VMEM((blocks, HEADS, ROWS), f32),
            pltpu.VMEM((blocks, HEADS, ROWS), f32),
            pltpu.VMEM((blocks, HEADS, ROWS), f32),
            pltpu.VMEM((HEADS, ROWS), f32),
            pltpu.VMEM((HEADS, WIDTH, ROWS), f32),
            pltpu.VMEM((ROWS, WIDTH), f32),
            pltpu.VMEM((ROWS, WIDTH), f32),
            pltpu.VMEM((blocks, 2, ROWS, WIDTH), bf16),
            pltpu.VMEM((blocks, 2, ROWS, WIDTH), bf16),
            pltpu.VMEM((2, ROWS, WIDTH), bf16),
            pltpu.VMEM((2, ROWS, WIDTH), bf16),
            pltpu.SemaphoreType.DMA((5,)),
            pltpu.SemaphoreType.DMA((REACH, CHUNKS)),
            pltpu.SemaphoreType.DMA((REACH, CHUNKS)),
            pltpu.SemaphoreType.DMA((REACH, CHUNKS)),
            pltpu.SemaphoreType.DMA((REACH, CHUNKS)),
            pltpu.SemaphoreType.DMA((4, CHUNKS)),
            pltpu.SemaphoreType.DMA((4, CHUNKS)),
        ],
        compiler_params=pltpu.CompilerParams(
            collective_id=0, has_side_effects=True, vmem_limit_bytes=48 * 1024 * 1024
        ),
    )(*operands)
    return pl.pallas_call(
        store_kernel,
        out_shape=results,
        in_specs=[in_vmem] * 3,
        out_specs=[in_hbm] * 3,
        scratch_shapes=[pltpu.SemaphoreType.DMA((3,))],
    )(*gradients)


def solution(mesh):
    rows = P(("dp", "ctx"), None)
    return jax.shard_map(
        shards,
        mesh=mesh,
        in_specs=(rows, rows, rows, rows, P("dp")),
        out_specs=(rows, rows, rows),
        check_vma=False,
    )
```

time: 48.4 us -> 48.2 us (level); the launches traced: 48.1 us -> 47.3 us
  local copies, waits for them, and re-layouts: 6.46 us -> 2.02 us
  Pallas kernels: 41 us -> 44.7 us
    unnamed x13 -> x6, local copies, waits for them, and re-layouts: 6.46 us -> 2.02 us
    pallas_call x1 -> x2, Pallas kernels: 41 us -> 44.7 us  [the longest x1 42.7 us: shards(): pl.pallas_call(attention_kernel, out_shape=results, in_specs=[in_hbm] * 5...]
where the time goes in v2:
time: 48.2 us; the launch traced here: 47.3 us
  Pallas kernels  44.7 us (93%)
  local copies, waits for them, and re-layouts  2.02 us (4%)
  between operations  0.65 us (1%)
    pallas_call x1, Pallas kernels, shards(): pl.pallas_call(attention_kernel, out_shape=results, in_specs=[in_hbm] * 5...  42.7 us
    unnamed x6, local copies, waits for them, and re-layouts  2.02 us
    pallas_call x1, Pallas kernels, shards(): pl.pallas_call(store_kernel, out_shape=results, in_specs=[in_vmem] * 3, o...  1.93 us

profile of v2, /device:TPU:22, one launch (start us, length us, event | category | flops | bytes accessed | tf_op | source)
XLA Modules:
  0.0 47.3 jit_solution(5556556173803746247)
XLA Ops:
  0.6 42.7 %shard_map.76 = (bf16[256,1024]{1,0:T(8,128)(2,1)S(1)}, bf16[256,128]{1,0:T(8,128)(2,1)S(1)}, bf16[256,128]{1,0:T(8,128)(2,1)S(1)}) custom-call(s32[16]{0:T(128)} %lengths_hbm.1, bf16[256,1024]{1,0:T(8,128)(2,1)} %q_hbm.1, bf16[256,128]{1,0:T(8,128)(2,1)} %k_hbm.1, bf16[256,128]{1,0:T(8,128)(2,1)} %v_hbm.1, bf16[256,1024]{1,0:T(8,128)(2,1)} %o_hbm.1), custom_call_target="tpu_custom_call" | custom-call | tf_op jit(solution)/shard_map/pallas_call | solution.py:381
  43.4 0.0 copy-start
  43.4 0.8 %copy-done = bf16[256,1024]{1,0:T(8,128)(2,1)} copy-done((bf16[256,1024]{1,0:T(8,128)(2,1)}, bf16[256,1024]{1,0:T(8,128)(2,1)S(1)}, u32[]{:S(2)}) %copy-start) | copy-done | bytes 524312
  44.2 0.0 copy-start.1
  44.2 0.6 %copy-done.1 = bf16[256,128]{1,0:T(8,128)(2,1)} copy-done((bf16[256,128]{1,0:T(8,128)(2,1)}, bf16[256,128]{1,0:T(8,128)(2,1)S(1)}, u32[]{:S(2)}) %copy-start.1) | copy-done | bytes 65560
  44.8 0.0 copy-start.2
  44.8 0.6 %copy-done.2 = bf16[256,128]{1,0:T(8,128)(2,1)} copy-done((bf16[256,128]{1,0:T(8,128)(2,1)}, bf16[256,128]{1,0:T(8,128)(2,1)S(1)}, u32[]{:S(2)}) %copy-start.2) | copy-done | bytes 65560
  45.4 1.9 %shard_map.77 = (bf16[256,1024]{1,0:T(8,128)(2,1)}, bf16[256,128]{1,0:T(8,128)(2,1)}, bf16[256,128]{1,0:T(8,128)(2,1)}) custom-call(bf16[256,1024]{1,0:T(8,128)(2,1)} %copy-done, bf16[256,128]{1,0:T(8,128)(2,1)} %copy-done.1, bf16[256,128]{1,0:T(8,128)(2,1)} %copy-done.2), custom_call_target="tpu_custom_call" | custom-call | tf_op jit(solution)/shard_map/pallas_call | solution.py:421
Async XLA Ops:
  43.4 0.8 %copy-start = (bf16[256,1024]{1,0:T(8,128)(2,1)}, bf16[256,1024]{1,0:T(8,128)(2,1)S(1)}, u32[]{:S(2)}) copy-start(bf16[256,1024]{1,0:T(8,128)(2,1)S(1)} %get-tuple-element.6.dq) | copy-start | bytes 1572868
  44.2 0.6 %copy-start.1 = (bf16[256,128]{1,0:T(8,128)(2,1)}, bf16[256,128]{1,0:T(8,128)(2,1)S(1)}, u32[]{:S(2)}) copy-start(bf16[256,128]{1,0:T(8,128)(2,1)S(1)} %get-tuple-element.7.dk) | copy-start | bytes 196612
  44.8 0.6 %copy-start.2 = (bf16[256,128]{1,0:T(8,128)(2,1)}, bf16[256,128]{1,0:T(8,128)(2,1)S(1)}, u32[]{:S(2)}) copy-start(bf16[256,128]{1,0:T(8,128)(2,1)S(1)} %get-tuple-element.8.dv) | copy-start | bytes 196612

commit v3 on v2

--- a/solution.py
+++ b/solution.py
@@ -18,6 +18,7 @@
 FIRST = 4
 DOCS = 16
 CHUNKS = 4
+FAR = ()
 
 
 def attention_kernel(
@@ -67,19 +68,19 @@
     left = jnp.maximum(me - 1, 0)
     right = jnp.minimum(me + 1, size - 1)
 
-    out_far = (me >= 4) & (me < 12)
+    out_far = ((me >= 4) & (me < 12)) & bool(FAR)
     out_relay = jnp.where(me < 6, me - 2, jnp.where(me < 10, me + 6, me - 10))
-    is_relay = (me < 4) | (me >= 12)
+    is_relay = ((me < 4) | (me >= 12)) & bool(FAR)
     relay_from = jnp.where(me < 2, me + 10, jnp.where(me < 4, me + 2, me - 6))
     relay_to = jnp.where(me < 2, me + 14, jnp.where(me < 4, me + 6, me - 2))
-    in_far = me >= 8
+    in_far = (me >= 8) & bool(FAR)
     in_relay = jnp.where(me < 10, me - 6, jnp.where(me < 14, me + 2, me - 14))
-    back_far = me >= 8
+    back_far = (me >= 8) & bool(FAR)
     back_relay = jnp.where(me < 14, me - 6, me - 14)
-    is_back_relay = me < 8
+    is_back_relay = (me < 8) & bool(FAR)
     back_relay_from = jnp.where(me < 2, me + 14, me + 6)
     back_relay_to = jnp.where(me < 2, me + 10, me + 2)
-    in_back = (me >= 4) & (me < 12)
+    in_back = ((me >= 4) & (me < 12)) & bool(FAR)
     in_back_relay = jnp.where(me < 10, me - 2, me - 10)
 
     loads = [
@@ -141,17 +142,20 @@
             forward(k, c).start()
 
     def relay(c):
-        @pl.when(is_relay)
-        def _():
-            to_relay(c).wait_recv()
-            from_relay(c).start()
+        if c in FAR:
+
+            @pl.when(is_relay)
+            def _():
+                to_relay(c).wait_recv()
+                from_relay(c).start()
 
     for c in range(CHUNKS):
         send_forward(0, c)
-
-        @pl.when(out_far)
-        def _(c=c):
-            to_relay(c).start()
+        if c in FAR:
+
+            @pl.when(out_far)
+            def _(c=c):
+                to_relay(c).start()
 
     loads[0].wait()
     places = me * ROWS + lax.broadcasted_iota(jnp.int32, (8, ROWS), 1)
@@ -206,11 +210,11 @@
 
     def arrive(k, c):
         def step():
-            if k == REACH:
+            if k == REACH and c in FAR:
                 from_relay(c).wait_recv()
             else:
                 forward(k - 1, c).wait_recv()
-                if k < REACH - 1:
+                if k < REACH - 1 or (k == REACH - 1 and c not in FAR):
                     send_forward(k, c)
 
         return step
@@ -296,24 +300,25 @@
         @pl.when(condition)
         def _():
             for c in chunks:
-                back_to_relay(c).wait_recv()
-                back_from_relay(c).start()
+                if c in FAR:
+                    back_to_relay(c).wait_recv()
+                    back_from_relay(c).start()
 
     def pass_back(k):
         for c in range(CHUNKS):
             part, rows = piece(c)
             own = own_parts[part]
-            if k < REACH - 1:
-
-                @pl.when(has_right)
+            if k < REACH - 1 or (k == REACH - 1 and c not in FAR):
+
+                @pl.when(has_right & (depth + 1 > k))
                 def _(c=c, part=part, rows=rows, own=own):
                     send_back(k + 1, c).wait_recv()
                     own[rows] += recv_box[k, part, rows].astype(jnp.float32)
 
             send_box[k, part, rows] = own[rows].astype(jnp.bfloat16)
-            (back_to_relay(c) if k == REACH else send_back(k, c)).start()
-
-    for k in (3, 4, 2):
+            (back_to_relay(c) if k == REACH and c in FAR else send_back(k, c)).start()
+
+    for k in (4, 3, 2):
         when_reached(k, lambda k=k: gradients(k), lambda k=k: pass_back(k))
     relay_back((me >= 4) & (me < 8), (0, 1))
     when_reached(1, lambda: gradients(1), lambda: pass_back(1))
@@ -333,7 +338,7 @@
 
     @pl.when(in_back)
     def _():
-        for c in range(CHUNKS):
+        for c in FAR:
             part, rows = piece(c)
             back_from_relay(c).wait_recv()
             own_parts[part][rows] += far_box[part, rows].astype(jnp.float32)
@@ -341,19 +346,20 @@
     dv_out[...] = value_part[...].astype(jnp.bfloat16)
     dk_out[...] = (key_part[...] * score_scale).astype(jnp.bfloat16)
 
-    def sent(condition, copy):
+    def sent(condition, copy, chunks):
         @pl.when(condition)
         def _():
-            for c in range(CHUNKS):
+            for c in chunks:
                 copy(c).wait_send()
 
-    for k in range(REACH - 1):
-        sent(has_right & (depth >= k), functools.partial(forward, k))
-        sent(depth >= k + 1, functools.partial(send_back, k + 1))
-    sent(out_far, to_relay)
-    sent(is_relay, from_relay)
-    sent(back_far, back_to_relay)
-    sent(is_back_relay, back_from_relay)
+    for k in range(REACH):
+        chunks = [c for c in range(CHUNKS) if k < REACH - 1 or c not in FAR]
+        sent(has_right & (depth >= k), functools.partial(forward, k), chunks)
+        sent(depth >= k + 1, functools.partial(send_back, k + 1), chunks)
+    sent(out_far, to_relay, FAR)
+    sent(is_relay, from_relay, FAR)
+    sent(back_far, back_to_relay, FAR)
+    sent(is_back_relay, back_from_relay, FAR)
 
 
 def store_kernel(dq, dk, dv, dq_out, dk_out, dv_out, sem):
@@ -407,10 +413,10 @@
             pltpu.VMEM((2, ROWS, WIDTH), bf16),
             pltpu.VMEM((2, ROWS, WIDTH), bf16),
             pltpu.SemaphoreType.DMA((5,)),
-            pltpu.SemaphoreType.DMA((REACH, CHUNKS)),
-            pltpu.SemaphoreType.DMA((REACH, CHUNKS)),
-            pltpu.SemaphoreType.DMA((REACH, CHUNKS)),
-            pltpu.SemaphoreType.DMA((REACH, CHUNKS)),
+            pltpu.SemaphoreType.DMA((blocks, CHUNKS)),
+            pltpu.SemaphoreType.DMA((blocks, CHUNKS)),
+            pltpu.SemaphoreType.DMA((blocks, CHUNKS)),
+            pltpu.SemaphoreType.DMA((blocks, CHUNKS)),
             pltpu.SemaphoreType.DMA((4, CHUNKS)),
             pltpu.SemaphoreType.DMA((4, CHUNKS)),
         ],
@@ -418,6 +424,7 @@
             collective_id=0, has_side_effects=True, vmem_limit_bytes=48 * 1024 * 1024
         ),
     )(*operands)
+    gradients = [pltpu.with_memory_space_constraint(g, pltpu.VMEM) for g in gradients]
     return pl.pallas_call(
         store_kernel,
         out_shape=results,

time: 48.2 us -> 40.7 us (0.84); the launches traced: 47.3 us -> 40.6 us
  Pallas kernels: 44.7 us -> 40 us
  local copies, waits for them, and re-layouts: 2.02 us -> 0 us
    pallas_call x1, Pallas kernels: 42.7 us -> 39.1 us  [shards(): pl.pallas_call(attention_kernel, out_shape=results, in_specs=[in_hbm] * 5...]
    unnamed x6 -> x0, local copies, waits for them, and re-layouts: 2.02 us -> none
    pallas_call x1, Pallas kernels: 1.93 us -> 0.85 us  [shards(): pl.pallas_call(store_kernel, out_shape=results, in_specs=[in_vmem] * 3, o...]
where the time goes in v3:
time: 40.7 us; the launch traced here: 40.6 us
  Pallas kernels  40 us (98%)
  between operations  0.64 us (2%)
    pallas_call x1, Pallas kernels, shards(): pl.pallas_call(attention_kernel, out_shape=results, in_specs=[in_hbm] * 5...  39.1 us
    pallas_call x1, Pallas kernels, shards(): pl.pallas_call(store_kernel, out_shape=results, in_specs=[in_vmem] * 3, o...  0.85 us

profile of v3, /device:TPU:22, one launch (start us, length us, event | category | flops | bytes accessed | tf_op | source)
XLA Modules:
  0.0 40.6 jit_solution(13099482688482949554)
XLA Ops:
  0.6 39.1 %shard_map.76 = (bf16[256,1024]{1,0:T(8,128)(2,1)S(1)}, bf16[256,128]{1,0:T(8,128)(2,1)S(1)}, bf16[256,128]{1,0:T(8,128)(2,1)S(1)}) custom-call(s32[16]{0:T(128)} %lengths_hbm.1, bf16[256,1024]{1,0:T(8,128)(2,1)} %q_hbm.1, bf16[256,128]{1,0:T(8,128)(2,1)} %k_hbm.1, bf16[256,128]{1,0:T(8,128)(2,1)} %v_hbm.1, bf16[256,1024]{1,0:T(8,128)(2,1)} %o_hbm.1), custom_call_target="tpu_custom_call" | custom-call | tf_op jit(solution)/shard_map/pallas_call | solution.py:387
  39.7 0.9 %shard_map.77 = (bf16[256,1024]{1,0:T(8,128)(2,1)}, bf16[256,128]{1,0:T(8,128)(2,1)}, bf16[256,128]{1,0:T(8,128)(2,1)}) custom-call(bf16[256,1024]{1,0:T(8,128)(2,1)S(1)} %get-tuple-element.6.dq, bf16[256,128]{1,0:T(8,128)(2,1)S(1)} %get-tuple-element.7.dk, bf16[256,128]{1,0:T(8,128)(2,1)S(1)} %get-tuple-element.8.dv), custom_call_target="tpu_custom_call" | custom-call | tf_op jit(solution)/shard_map/pallas_call | solution.py:428

commit v4 on v2

--- a/solution.py
+++ b/solution.py
@@ -34,6 +34,7 @@
     o_ref,
     keys,
     values,
+    picked,
     passing,
     keys_turned,
     bias,
@@ -50,7 +51,7 @@
     send_box,
     recv_box,
     far_box,
-    passing_back,
+    pair_box,
     load_sem,
     kv_send_sem,
     kv_recv_sem,
@@ -67,20 +68,15 @@
     left = jnp.maximum(me - 1, 0)
     right = jnp.minimum(me + 1, size - 1)
 
-    out_far = (me >= 4) & (me < 12)
-    out_relay = jnp.where(me < 6, me - 2, jnp.where(me < 10, me + 6, me - 10))
-    is_relay = (me < 4) | (me >= 12)
-    relay_from = jnp.where(me < 2, me + 10, jnp.where(me < 4, me + 2, me - 6))
-    relay_to = jnp.where(me < 2, me + 14, jnp.where(me < 4, me + 6, me - 2))
-    in_far = me >= 8
-    in_relay = jnp.where(me < 10, me - 6, jnp.where(me < 14, me + 2, me - 14))
-    back_far = me >= 8
-    back_relay = jnp.where(me < 14, me - 6, me - 14)
-    is_back_relay = me < 8
-    back_relay_from = jnp.where(me < 2, me + 14, me + 6)
-    back_relay_to = jnp.where(me < 2, me + 10, me + 2)
-    in_back = (me >= 4) & (me < 12)
-    in_back_relay = jnp.where(me < 10, me - 2, me - 10)
+    odd = me % 2 == 1
+    picks = odd & (me >= 5) & (me <= 11)
+    pick_relay = jnp.where(me == 5, 10, jnp.where(me == 7, 5, jnp.where(me == 9, 14, 0)))
+    is_relay = (me == 10) | (me == 5) | (me == 14) | (me == 0)
+    picked_on = jnp.where(me == 10, 5, jnp.where(me == 5, 7, jnp.where(me == 14, 9, 11)))
+    relay_to = jnp.where(me == 0, 15, jnp.where(me == 5, 11, me - 1))
+    in_relay = jnp.where(me < 10, 10, jnp.where(me < 12, 5, jnp.where(me < 14, 14, 0)))
+    is_far = me >= 8
+    owns_far = (me >= 4) & (me < 12)
 
     loads = [
         pltpu.make_async_copy(lengths_hbm, lengths, load_sem.at[4]),
@@ -101,11 +97,9 @@
 
     greet(has_left, left)
     greet(has_right, right)
-    greet(is_relay, relay_from)
-    greet(in_far, in_relay)
-    greet(is_back_relay, back_relay_from)
-    greet(in_back, in_back_relay)
-    targets = (has_left, has_right, out_far, is_relay, back_far, is_back_relay)
+    greet(is_relay, picked_on)
+    greet(is_far & (me != 9) & (me != 13), in_relay)
+    targets = (has_left, has_right, picks, is_relay, (me == 0) | (me == 5))
     pl.semaphore_wait(barrier, sum(target.astype(jnp.int32) for target in targets))
 
     def remote(source, target, send, recv, device):
@@ -128,12 +122,19 @@
 
     def to_relay(c):
         part, rows = piece(c)
-        return remote(own_piece(c), passing.at[part, rows], far_send_sem.at[0, c], far_recv_sem.at[0, c], out_relay)
-
-    def from_relay(c):
-        part, rows = piece(c)
-        target = (keys, values)[part].at[REACH, rows]
-        return remote(passing.at[part, rows], target, far_send_sem.at[1, c], far_recv_sem.at[1, c], relay_to)
+        return remote(
+            picked.at[part, rows], passing.at[part, rows], far_send_sem.at[0, c], far_recv_sem.at[0, c], pick_relay
+        )
+
+    def from_relay(c, which):
+        part, rows = piece(c)
+        return remote(
+            passing.at[part, rows],
+            (keys, values)[part].at[REACH, rows],
+            far_send_sem.at[1 + which, c],
+            far_recv_sem.at[1, c],
+            relay_to - which,
+        )
 
     def send_forward(k, c):
         @pl.when(has_right & (depth >= k))
@@ -144,14 +145,11 @@
         @pl.when(is_relay)
         def _():
             to_relay(c).wait_recv()
-            from_relay(c).start()
+            for which in (1, 0):
+                from_relay(c, which).start()
 
     for c in range(CHUNKS):
         send_forward(0, c)
-
-        @pl.when(out_far)
-        def _(c=c):
-            to_relay(c).start()
 
     loads[0].wait()
     places = me * ROWS + lax.broadcasted_iota(jnp.int32, (8, ROWS), 1)
@@ -165,6 +163,13 @@
         key_places = (me - k) * ROWS + lax.broadcasted_iota(jnp.int32, (ROWS, ROWS), 0)
         allowed = (key_places >= starts) & (key_places <= places)
         bias[k] = jnp.where(allowed, 0.0, MASKED)
+
+    def far_in_use(block):
+        start, end = jnp.int32(0), jnp.int32(0)
+        for d in range(DOCS):
+            end = end + lengths[d]
+            start = jnp.where(end <= (block + REACH) * ROWS, end, start)
+        return jnp.full((HALF, WIDTH), start, jnp.int32) < (block + 1) * ROWS
 
     to_log2 = math.log2(math.e) / math.sqrt(WIDTH)
     score_scale = 1.0 / math.sqrt(WIDTH)
@@ -207,13 +212,20 @@
     def arrive(k, c):
         def step():
             if k == REACH:
-                from_relay(c).wait_recv()
+                from_relay(c, 0).wait_recv()
             else:
                 forward(k - 1, c).wait_recv()
                 if k < REACH - 1:
                     send_forward(k, c)
 
         return step
+
+    def pick(c):
+        part, rows = piece(c)
+        place = (keys, values)[part]
+        before, own = (place[k, rows].astype(jnp.float32) for k in (1, 0))
+        picked[part, rows] = jnp.where(far_in_use(me - 1), before, own).astype(jnp.bfloat16)
+        to_relay(c).start()
 
     loads[1].wait()
     loads[3].wait()
@@ -222,25 +234,28 @@
     loads[4].wait()
     grad_dots(0)
 
-    when_reached(1, arrive(1, 0), arrive(1, 1))
+    for c in range(CHUNKS):
+        when_reached(1, arrive(1, c))
+
+        @pl.when(picks)
+        def _(c=c):
+            pick(c)
+
+    when_reached(1, lambda: scores(1))
     relay(0)
-    when_reached(1, arrive(1, 2), arrive(1, 3))
+    when_reached(2, arrive(2, 0), arrive(2, 1))
     relay(1)
-    when_reached(1, lambda: scores(1))
-    when_reached(2, arrive(2, 0), arrive(2, 1))
+    when_reached(2, arrive(2, 2))
     relay(2)
+    when_reached(2, arrive(2, 3))
+    relay(3)
     when_reached(1, lambda: grad_dots(1))
-    when_reached(2, arrive(2, 2), arrive(2, 3))
-    relay(3)
     when_reached(2, lambda: scores(2))
-    when_reached(3, arrive(3, 0), arrive(3, 1), lambda: grad_dots(2), lambda: scores(3))
-
-    @pl.when(depth == 2)
-    def _():
-        grad_dots(2)
-
+    when_reached(3, arrive(3, 0), arrive(3, 1), lambda: scores(3))
+    when_reached(2, lambda: grad_dots(2))
+    when_reached(4, arrive(4, 0), arrive(4, 1), lambda: scores(4))
     when_reached(3, arrive(3, 2), arrive(3, 3), lambda: grad_dots(3))
-    when_reached(4, arrive(4, 0), arrive(4, 1), lambda: scores(4), arrive(4, 2), arrive(4, 3), lambda: grad_dots(4))
+    when_reached(4, arrive(4, 2), arrive(4, 3), lambda: grad_dots(4))
 
     top = tops[0]
     for k in range(1, REACH + 1):
@@ -280,44 +295,69 @@
             send_box.at[k, part, rows], recv_box.at[k - 1, part, rows], grad_send_sem.at[k, c], grad_recv_sem.at[k - 1, c], left
         )
 
-    def back_to_relay(c):
+    def far_pair(c):
         part, rows = piece(c)
         return remote(
-            send_box.at[REACH, part, rows], passing_back.at[part, rows], far_send_sem.at[2, c], far_recv_sem.at[2, c], back_relay
-        )
-
-    def back_from_relay(c):
+            send_box.at[REACH, part, rows], pair_box.at[part, rows], far_send_sem.at[3, c], far_recv_sem.at[2, c], right
+        )
+
+    def far_back(c):
         part, rows = piece(c)
         return remote(
-            passing_back.at[part, rows], far_box.at[part, rows], far_send_sem.at[3, c], far_recv_sem.at[3, c], back_relay_to
-        )
-
-    def relay_back(condition, chunks):
-        @pl.when(condition)
-        def _():
-            for c in chunks:
-                back_to_relay(c).wait_recv()
-                back_from_relay(c).start()
-
-    def pass_back(k):
+            send_box.at[REACH, part, rows], far_box.at[part, rows], far_send_sem.at[3, c], far_recv_sem.at[3, c], me - 5
+        )
+
+    def far_on(c):
+        part, rows = piece(c)
+        return remote(far_box.at[part, rows], far_box.at[part, rows], far_send_sem.at[4, c], far_recv_sem.at[4, c], right)
+
+    def send_far():
         for c in range(CHUNKS):
             part, rows = piece(c)
-            own = own_parts[part]
-            if k < REACH - 1:
-
-                @pl.when(has_right)
-                def _(c=c, part=part, rows=rows, own=own):
-                    send_back(k + 1, c).wait_recv()
-                    own[rows] += recv_box[k, part, rows].astype(jnp.float32)
-
-            send_box[k, part, rows] = own[rows].astype(jnp.bfloat16)
-            (back_to_relay(c) if k == REACH else send_back(k, c)).start()
-
-    for k in (3, 4, 2):
-        when_reached(k, lambda k=k: gradients(k), lambda k=k: pass_back(k))
-    relay_back((me >= 4) & (me < 8), (0, 1))
-    when_reached(1, lambda: gradients(1), lambda: pass_back(1))
-    relay_back((me >= 4) & (me < 8), (2, 3))
+            send_box[REACH, part, rows] = own_parts[part][rows].astype(jnp.bfloat16)
+
+            @pl.when(jnp.logical_not(odd))
+            def _(c=c):
+                far_pair(c).start()
+
+    def add_pair(c):
+        @pl.when(is_far & odd)
+        def _():
+            part, rows = piece(c)
+            far_pair(c).wait_recv()
+            pair = send_box[REACH, part, rows].astype(jnp.float32) + pair_box[part, rows].astype(jnp.float32)
+            send_box[REACH, part, rows] = pair.astype(jnp.bfloat16)
+            far_back(c).start()
+
+    def pass_far(c):
+        @pl.when(owns_far & jnp.logical_not(odd))
+        def _():
+            far_back(c).wait_recv()
+            far_on(c).start()
+
+    def pass_back(k, c):
+        part, rows = piece(c)
+        own = own_parts[part]
+        if k < REACH - 1:
+
+            @pl.when(has_right)
+            def _():
+                send_back(k + 1, c).wait_recv()
+                own[rows] += recv_box[k, part, rows].astype(jnp.float32)
+
+        send_box[k, part, rows] = own[rows].astype(jnp.bfloat16)
+        send_back(k, c).start()
+
+    when_reached(4, lambda: gradients(4), send_far)
+    when_reached(3, lambda: gradients(3), *[functools.partial(pass_back, 3, c) for c in range(CHUNKS)])
+    when_reached(2, lambda: gradients(2))
+    for c in range(CHUNKS):
+        add_pair(c)
+        when_reached(2, functools.partial(pass_back, 2, c))
+    when_reached(1, lambda: gradients(1))
+    for c in range(CHUNKS):
+        when_reached(1, functools.partial(pass_back, 1, c))
+        pass_far(c)
     gradients(0)
     for h in range(HEADS):
         dq_out[:, h * WIDTH : (h + 1) * WIDTH] = (dq_acc[h] * score_scale).T.astype(jnp.bfloat16)
@@ -329,14 +369,17 @@
             send_back(1, c).wait_recv()
             own_parts[part][rows] += recv_box[0, part, rows].astype(jnp.float32)
 
-    relay_back(me < 4, range(CHUNKS))
-
-    @pl.when(in_back)
+    @pl.when(owns_far)
     def _():
+        in_use = far_in_use(me)
         for c in range(CHUNKS):
             part, rows = piece(c)
-            back_from_relay(c).wait_recv()
-            own_parts[part][rows] += far_box[part, rows].astype(jnp.float32)
+
+            @pl.when(odd)
+            def _(c=c):
+                far_on(c).wait_recv()
+
+            own_parts[part][rows] += jnp.where(in_use, far_box[part, rows].astype(jnp.float32), 0.0)
 
     dv_out[...] = value_part[...].astype(jnp.bfloat16)
     dk_out[...] = (key_part[...] * score_scale).astype(jnp.bfloat16)
@@ -350,10 +393,12 @@
     for k in range(REACH - 1):
         sent(has_right & (depth >= k), functools.partial(forward, k))
         sent(depth >= k + 1, functools.partial(send_back, k + 1))
-    sent(out_far, to_relay)
-    sent(is_relay, from_relay)
-    sent(back_far, back_to_relay)
-    sent(is_back_relay, back_from_relay)
+    sent(picks, to_relay)
+    sent(is_relay, functools.partial(from_relay, which=0))
+    sent(is_relay, functools.partial(from_relay, which=1))
+    sent(is_far & jnp.logical_not(odd), far_pair)
+    sent(is_far & odd, far_back)
+    sent(owns_far & jnp.logical_not(odd), far_on)
 
 
 def store_kernel(dq, dk, dv, dq_out, dk_out, dv_out, sem):
@@ -390,6 +435,7 @@
             pltpu.VMEM((blocks, ROWS, WIDTH), bf16),
             pltpu.VMEM((blocks, ROWS, WIDTH), bf16),
             pltpu.VMEM((2, ROWS, WIDTH), bf16),
+            pltpu.VMEM((2, ROWS, WIDTH), bf16),
             pltpu.VMEM((blocks, WIDTH, ROWS), bf16),
             pltpu.VMEM((blocks, ROWS, ROWS), f32),
             pltpu.VMEM((blocks, HEADS, ROWS, ROWS), f32),
@@ -407,17 +453,18 @@
             pltpu.VMEM((2, ROWS, WIDTH), bf16),
             pltpu.VMEM((2, ROWS, WIDTH), bf16),
             pltpu.SemaphoreType.DMA((5,)),
-            pltpu.SemaphoreType.DMA((REACH, CHUNKS)),
-            pltpu.SemaphoreType.DMA((REACH, CHUNKS)),
-            pltpu.SemaphoreType.DMA((REACH, CHUNKS)),
-            pltpu.SemaphoreType.DMA((REACH, CHUNKS)),
-            pltpu.SemaphoreType.DMA((4, CHUNKS)),
-            pltpu.SemaphoreType.DMA((4, CHUNKS)),
+            pltpu.SemaphoreType.DMA((blocks, CHUNKS)),
+            pltpu.SemaphoreType.DMA((blocks, CHUNKS)),
+            pltpu.SemaphoreType.DMA((blocks, CHUNKS)),
+            pltpu.SemaphoreType.DMA((blocks, CHUNKS)),
+            pltpu.SemaphoreType.DMA((5, CHUNKS)),
+            pltpu.SemaphoreType.DMA((5, CHUNKS)),
         ],
         compiler_params=pltpu.CompilerParams(
             collective_id=0, has_side_effects=True, vmem_limit_bytes=48 * 1024 * 1024
         ),
     )(*operands)
+    gradients = [pltpu.with_memory_space_constraint(g, pltpu.VMEM) for g in gradients]
     return pl.pallas_call(
         store_kernel,
         out_shape=results,

time: 48.2 us -> 39 us (0.81)
  the two profiles are of different devices: /device:TPU:22 before, /device:TPU:52 now
where the time goes in v4:
time: 39 us; the launch traced here: 38.9 us
  Pallas kernels  38.2 us (98%)
  between operations  0.64 us (2%)
    pallas_call x1, Pallas kernels, shards(): pl.pallas_call(attention_kernel, out_shape=results, in_specs=[in_hbm] * 5...  37.4 us
    pallas_call x1, Pallas kernels, shards(): pl.pallas_call(store_kernel, out_shape=results, in_specs=[in_vmem] * 3, o...  0.85 us

profile of v4, /device:TPU:52, one launch (start us, length us, event | category | flops | bytes accessed | tf_op | source)
XLA Modules:
  0.0 38.9 jit_solution(2448702423198409354)
XLA Ops:
  0.6 37.4 %shard_map.76 = (bf16[256,1024]{1,0:T(8,128)(2,1)S(1)}, bf16[256,128]{1,0:T(8,128)(2,1)S(1)}, bf16[256,128]{1,0:T(8,128)(2,1)S(1)}) custom-call(s32[16]{0:T(128)} %lengths_hbm.1, bf16[256,1024]{1,0:T(8,128)(2,1)} %q_hbm.1, bf16[256,128]{1,0:T(8,128)(2,1)} %k_hbm.1, bf16[256,128]{1,0:T(8,128)(2,1)} %v_hbm.1, bf16[256,1024]{1,0:T(8,128)(2,1)} %o_hbm.1), custom_call_target="tpu_custom_call" | custom-call | tf_op jit(solution)/shard_map/pallas_call | solution.py:426
  38.0 0.9 %shard_map.77 = (bf16[256,1024]{1,0:T(8,128)(2,1)}, bf16[256,128]{1,0:T(8,128)(2,1)}, bf16[256,128]{1,0:T(8,128)(2,1)}) custom-call(bf16[256,1024]{1,0:T(8,128)(2,1)S(1)} %get-tuple-element.6.dq, bf16[256,128]{1,0:T(8,128)(2,1)S(1)} %get-tuple-element.7.dk, bf16[256,128]{1,0:T(8,128)(2,1)S(1)} %get-tuple-element.8.dv), custom_call_target="tpu_custom_call" | custom-call | tf_op jit(solution)/shard_map/pallas_call | solution.py:468

commit v5 on v4

--- a/solution.py
+++ b/solution.py
@@ -13,11 +13,12 @@
 HEADS = 8
 WIDTH = 128
 ROWS = 256
-HALF = ROWS // 2
 REACH = 4
 FIRST = 4
 DOCS = 16
-CHUNKS = 4
+PIECES = 2
+CHUNKS = 2 * PIECES
+SLICE = ROWS // PIECES
 
 
 def attention_kernel(
@@ -59,6 +60,7 @@
     grad_recv_sem,
     far_send_sem,
     far_recv_sem,
+    far_ready,
 ):
     me = lax.axis_index("ctx")
     size = 16
@@ -72,11 +74,24 @@
     picks = odd & (me >= 5) & (me <= 11)
     pick_relay = jnp.where(me == 5, 10, jnp.where(me == 7, 5, jnp.where(me == 9, 14, 0)))
     is_relay = (me == 10) | (me == 5) | (me == 14) | (me == 0)
-    picked_on = jnp.where(me == 10, 5, jnp.where(me == 5, 7, jnp.where(me == 14, 9, 11)))
     relay_to = jnp.where(me == 0, 15, jnp.where(me == 5, 11, me - 1))
-    in_relay = jnp.where(me < 10, 10, jnp.where(me < 12, 5, jnp.where(me < 14, 14, 0)))
     is_far = me >= 8
     owns_far = (me >= 4) & (me < 12)
+
+    barrier = pltpu.get_barrier_semaphore()
+
+    def greet(condition, device):
+        @pl.when(condition)
+        def _():
+            pl.semaphore_signal(barrier, inc=1, device_id={"ctx": device}, device_id_type=MESH)
+
+    greet(has_left, left)
+    greet((me == 10) | (me == 11), 5)
+    greet(me == 5, 6)
+    greet(me == 8, 10)
+    greet(me == 9, 14)
+    greet(me == 0, 11)
+    greet((me == 14) | (me == 15), 0)
 
     loads = [
         pltpu.make_async_copy(lengths_hbm, lengths, load_sem.at[4]),
@@ -88,19 +103,17 @@
     for load in loads:
         load.start()
 
-    barrier = pltpu.get_barrier_semaphore()
-
-    def greet(condition, device):
-        @pl.when(condition)
-        def _():
-            pl.semaphore_signal(barrier, inc=1, device_id={"ctx": device}, device_id_type=MESH)
-
-    greet(has_left, left)
-    greet(has_right, right)
-    greet(is_relay, picked_on)
-    greet(is_far & (me != 9) & (me != 13), in_relay)
-    targets = (has_left, has_right, picks, is_relay, (me == 0) | (me == 5))
-    pl.semaphore_wait(barrier, sum(target.astype(jnp.int32) for target in targets))
+    expected = has_right.astype(jnp.int32)
+    for device, more in ((0, 2), (5, 2), (6, 1), (10, 1), (11, 1), (14, 1)):
+        expected += jnp.where(me == device, more, 0)
+
+    @pl.when(has_right)
+    def _():
+        pl.semaphore_wait(barrier, expected)
+
+    @pl.when(me == 14)
+    def _():
+        pl.semaphore_signal(far_ready, inc=1, device_id={"ctx": 9}, device_id_type=MESH)
 
     def remote(source, target, send, recv, device):
         return pltpu.make_async_remote_copy(
@@ -108,7 +121,7 @@
         )
 
     def piece(c):
-        return c // 2, pl.ds((c % 2) * HALF, HALF)
+        return c // PIECES, pl.ds((c % PIECES) * SLICE, SLICE)
 
     def own_piece(c):
         part, rows = piece(c)
@@ -169,7 +182,7 @@
         for d in range(DOCS):
             end = end + lengths[d]
             start = jnp.where(end <= (block + REACH) * ROWS, end, start)
-        return jnp.full((HALF, WIDTH), start, jnp.int32) < (block + 1) * ROWS
+        return jnp.full((SLICE, WIDTH), start, jnp.int32) < (block + 1) * ROWS
 
     to_log2 = math.log2(math.e) / math.sqrt(WIDTH)
     score_scale = 1.0 / math.sqrt(WIDTH)
@@ -225,6 +238,12 @@
         place = (keys, values)[part]
         before, own = (place[k, rows].astype(jnp.float32) for k in (1, 0))
         picked[part, rows] = jnp.where(far_in_use(me - 1), before, own).astype(jnp.bfloat16)
+        if c == 0:
+
+            @pl.when(me == 9)
+            def _():
+                pl.semaphore_wait(far_ready, 1)
+
         to_relay(c).start()
 
     loads[1].wait()
@@ -241,21 +260,18 @@
         def _(c=c):
             pick(c)
 
+    first, second = range(PIECES), range(PIECES, CHUNKS)
     when_reached(1, lambda: scores(1))
-    relay(0)
-    when_reached(2, arrive(2, 0), arrive(2, 1))
-    relay(1)
-    when_reached(2, arrive(2, 2))
-    relay(2)
-    when_reached(2, arrive(2, 3))
-    relay(3)
+    for c in range(CHUNKS):
+        when_reached(2, arrive(2, c))
+        relay(c)
     when_reached(1, lambda: grad_dots(1))
     when_reached(2, lambda: scores(2))
-    when_reached(3, arrive(3, 0), arrive(3, 1), lambda: scores(3))
+    when_reached(3, *[arrive(3, c) for c in first], lambda: scores(3))
     when_reached(2, lambda: grad_dots(2))
-    when_reached(4, arrive(4, 0), arrive(4, 1), lambda: scores(4))
-    when_reached(3, arrive(3, 2), arrive(3, 3), lambda: grad_dots(3))
-    when_reached(4, arrive(4, 2), arrive(4, 3), lambda: grad_dots(4))
+    when_reached(4, *[arrive(4, c) for c in first], lambda: scores(4))
+    when_reached(3, *[arrive(3, c) for c in second], lambda: grad_dots(3))
+    when_reached(4, *[arrive(4, c) for c in second], lambda: grad_dots(4))
 
     top = tops[0]
     for k in range(1, REACH + 1):
@@ -273,19 +289,25 @@
         factors[k] = factors[k] * inverse
     dq_acc[...] = jnp.zeros(dq_acc.shape, jnp.float32)
 
-    def gradients(k):
-        key_sum = jnp.zeros((ROWS, WIDTH), jnp.float32)
+    def value_gradients(k):
         value_sum = jnp.zeros((ROWS, WIDTH), jnp.float32)
         for h in range(HEADS):
+            soft_low = (weights[k, h] * factors[k, h : h + 1, :]).astype(jnp.bfloat16)
+            value_sum = value_sum + jnp.dot(soft_low, head(o_ref, h), preferred_element_type=jnp.float32)
+        value_part[...] = value_sum
+
+    def key_gradients(k):
+        key_sum = jnp.zeros((ROWS, WIDTH), jnp.float32)
+        for h in range(HEADS):
             soft = weights[k, h] * factors[k, h : h + 1, :]
-            score_grad = soft * (dots[k, h] - deltas[h : h + 1, :])
-            soft_low = soft.astype(jnp.bfloat16)
-            grad_low = score_grad.astype(jnp.bfloat16)
-            value_sum = value_sum + jnp.dot(soft_low, head(o_ref, h), preferred_element_type=jnp.float32)
+            grad_low = (soft * (dots[k, h] - deltas[h : h + 1, :])).astype(jnp.bfloat16)
             key_sum = key_sum + jnp.dot(grad_low, head(q_ref, h), preferred_element_type=jnp.float32)
             dq_acc[h] += jnp.dot(keys_turned[k], grad_low, preferred_element_type=jnp.float32)
-        value_part[...] = value_sum
         key_part[...] = key_sum
+
+    def gradients(k):
+        value_gradients(k)
+        key_gradients(k)
 
     own_parts = (value_part, key_part)
 
@@ -310,15 +332,6 @@
     def far_on(c):
         part, rows = piece(c)
         return remote(far_box.at[part, rows], far_box.at[part, rows], far_send_sem.at[4, c], far_recv_sem.at[4, c], right)
-
-    def send_far():
-        for c in range(CHUNKS):
-            part, rows = piece(c)
-            send_box[REACH, part, rows] = own_parts[part][rows].astype(jnp.bfloat16)
-
-            @pl.when(jnp.logical_not(odd))
-            def _(c=c):
-                far_pair(c).start()
 
     def add_pair(c):
         @pl.when(is_far & odd)
@@ -348,17 +361,35 @@
         send_box[k, part, rows] = own[rows].astype(jnp.bfloat16)
         send_back(k, c).start()
 
-    when_reached(4, lambda: gradients(4), send_far)
-    when_reached(3, lambda: gradients(3), *[functools.partial(pass_back, 3, c) for c in range(CHUNKS)])
-    when_reached(2, lambda: gradients(2))
-    for c in range(CHUNKS):
+    def passed(k, chunks):
+        return [functools.partial(pass_back, k, c) for c in chunks]
+
+    def send_far(chunks):
+        for c in chunks:
+            part, rows = piece(c)
+            send_box[REACH, part, rows] = own_parts[part][rows].astype(jnp.bfloat16)
+
+            @pl.when(jnp.logical_not(odd))
+            def _(c=c):
+                far_pair(c).start()
+
+    when_reached(3, lambda: value_gradients(3), *passed(3, first))
+    when_reached(4, lambda: value_gradients(4), lambda: send_far(first))
+    when_reached(3, lambda: key_gradients(3), *passed(3, second))
+    when_reached(4, lambda: key_gradients(4), lambda: send_far(second))
+    when_reached(2, lambda: gradients(2), *passed(2, first))
+    for c in first:
         add_pair(c)
-        when_reached(2, functools.partial(pass_back, 2, c))
+    when_reached(2, *passed(2, second))
     when_reached(1, lambda: gradients(1))
-    for c in range(CHUNKS):
-        when_reached(1, functools.partial(pass_back, 1, c))
+    for c in second:
+        add_pair(c)
+    when_reached(1, *passed(1, range(CHUNKS)))
+    for c in first:
         pass_far(c)
     gradients(0)
+    for c in second:
+        pass_far(c)
     for h in range(HEADS):
         dq_out[:, h * WIDTH : (h + 1) * WIDTH] = (dq_acc[h] * score_scale).T.astype(jnp.bfloat16)
 
@@ -459,6 +490,7 @@
             pltpu.SemaphoreType.DMA((blocks, CHUNKS)),
             pltpu.SemaphoreType.DMA((5, CHUNKS)),
             pltpu.SemaphoreType.DMA((5, CHUNKS)),
+            pltpu.SemaphoreType.REGULAR,
         ],
         compiler_params=pltpu.CompilerParams(
             collective_id=0, has_side_effects=True, vmem_limit_bytes=48 * 1024 * 1024

time: 39 us -> 37.6 us (0.964)
  the two profiles are of different devices: /device:TPU:52 before, /device:TPU:22 now
where the time goes in v5:
time: 37.6 us; the launch traced here: 36.9 us
  Pallas kernels  36.2 us (96%)
  between operations  0.64 us (2%)
    pallas_call x1, Pallas kernels, shards(): pl.pallas_call(attention_kernel, out_shape=results, in_specs=[in_hbm] * 5...  35.4 us
    pallas_call x1, Pallas kernels, shards(): pl.pallas_call(store_kernel, out_shape=results, in_specs=[in_vmem] * 3, o...  0.85 us

profile of v5, /device:TPU:22, one launch (start us, length us, event | category | flops | bytes accessed | tf_op | source)
XLA Modules:
  0.0 36.9 jit_solution(8663212305614038063)
XLA Ops:
  0.6 35.4 %shard_map.76 = (bf16[256,1024]{1,0:T(8,128)(2,1)S(1)}, bf16[256,128]{1,0:T(8,128)(2,1)S(1)}, bf16[256,128]{1,0:T(8,128)(2,1)S(1)}) custom-call(s32[16]{0:T(128)} %lengths_hbm.1, bf16[256,1024]{1,0:T(8,128)(2,1)} %q_hbm.1, bf16[256,128]{1,0:T(8,128)(2,1)} %k_hbm.1, bf16[256,128]{1,0:T(8,128)(2,1)} %v_hbm.1, bf16[256,1024]{1,0:T(8,128)(2,1)} %o_hbm.1), custom_call_target="tpu_custom_call" | custom-call | tf_op jit(solution)/shard_map/pallas_call | solution.py:457
  36.0 0.9 %shard_map.77 = (bf16[256,1024]{1,0:T(8,128)(2,1)}, bf16[256,128]{1,0:T(8,128)(2,1)}, bf16[256,128]{1,0:T(8,128)(2,1)}) custom-call(bf16[256,1024]{1,0:T(8,128)(2,1)S(1)} %get-tuple-element.6.dq, bf16[256,128]{1,0:T(8,128)(2,1)S(1)} %get-tuple-element.7.dk, bf16[256,128]{1,0:T(8,128)(2,1)S(1)} %get-tuple-element.8.dv), custom_call_target="tpu_custom_call" | custom-call | tf_op jit(solution)/shard_map/pallas_call | solution.py:500

commit v6 on v5

--- a/solution.py
+++ b/solution.py
@@ -373,17 +373,16 @@
             def _(c=c):
                 far_pair(c).start()
 
+    when_reached(4, lambda: value_gradients(4), lambda: send_far(first))
     when_reached(3, lambda: value_gradients(3), *passed(3, first))
-    when_reached(4, lambda: value_gradients(4), lambda: send_far(first))
+    when_reached(4, lambda: key_gradients(4), lambda: send_far(second))
     when_reached(3, lambda: key_gradients(3), *passed(3, second))
-    when_reached(4, lambda: key_gradients(4), lambda: send_far(second))
-    when_reached(2, lambda: gradients(2), *passed(2, first))
-    for c in first:
-        add_pair(c)
-    when_reached(2, *passed(2, second))
+    when_reached(2, lambda: gradients(2))
+    for chunks in (first, second):
+        for c in chunks:
+            add_pair(c)
+        when_reached(2, *passed(2, chunks))
     when_reached(1, lambda: gradients(1))
-    for c in second:
-        add_pair(c)
     when_reached(1, *passed(1, range(CHUNKS)))
     for c in first:
         pass_far(c)

time: 37.6 us -> 36.4 us (0.968)
  Pallas kernels: 36.2 us -> 35.2 us
    pallas_call x1, Pallas kernels: 35.4 us -> 34.4 us  [shards(): pl.pallas_call(attention_kernel, out_shape=results, in_specs=[in_hbm] * 5...]
where the time goes in v6:
time: 36.4 us; the launch traced here: 35.9 us
  Pallas kernels  35.2 us (97%)
  between operations  0.64 us (2%)
    pallas_call x1, Pallas kernels, shards(): pl.pallas_call(attention_kernel, out_shape=results, in_specs=[in_hbm] * 5...  34.4 us
    pallas_call x1, Pallas kernels, shards(): pl.pallas_call(store_kernel, out_shape=results, in_specs=[in_vmem] * 3, o...  0.85 us

profile of v6, /device:TPU:22, one launch (start us, length us, event | category | flops | bytes accessed | tf_op | source)
XLA Modules:
  0.0 35.9 jit_solution(8808578088202339163)
XLA Ops:
  0.6 34.4 %shard_map.76 = (bf16[256,1024]{1,0:T(8,128)(2,1)S(1)}, bf16[256,128]{1,0:T(8,128)(2,1)S(1)}, bf16[256,128]{1,0:T(8,128)(2,1)S(1)}) custom-call(s32[16]{0:T(128)} %lengths_hbm.1, bf16[256,1024]{1,0:T(8,128)(2,1)} %q_hbm.1, bf16[256,128]{1,0:T(8,128)(2,1)} %k_hbm.1, bf16[256,128]{1,0:T(8,128)(2,1)} %v_hbm.1, bf16[256,1024]{1,0:T(8,128)(2,1)} %o_hbm.1), custom_call_target="tpu_custom_call" | custom-call | tf_op jit(solution)/shard_map/pallas_call | solution.py:456
  35.0 0.9 %shard_map.77 = (bf16[256,1024]{1,0:T(8,128)(2,1)}, bf16[256,128]{1,0:T(8,128)(2,1)}, bf16[256,128]{1,0:T(8,128)(2,1)}) custom-call(bf16[256,1024]{1,0:T(8,128)(2,1)S(1)} %get-tuple-element.6.dq, bf16[256,128]{1,0:T(8,128)(2,1)S(1)} %get-tuple-element.7.dk, bf16[256,128]{1,0:T(8,128)(2,1)S(1)} %get-tuple-element.8.dv), custom_call_target="tpu_custom_call" | custom-call | tf_op jit(solution)/shard_map/pallas_call | solution.py:499

commit v7 on v6

--- a/solution.py
+++ b/solution.py
@@ -72,9 +72,9 @@
 
     odd = me % 2 == 1
     picks = odd & (me >= 5) & (me <= 11)
-    pick_relay = jnp.where(me == 5, 10, jnp.where(me == 7, 5, jnp.where(me == 9, 14, 0)))
-    is_relay = (me == 10) | (me == 5) | (me == 14) | (me == 0)
-    relay_to = jnp.where(me == 0, 15, jnp.where(me == 5, 11, me - 1))
+    pick_relay = jnp.where(me == 5, 10, jnp.where(me == 7, 5, jnp.where(me == 9, 15, 0)))
+    is_relay = (me == 10) | (me == 5) | (me == 15) | (me == 0)
+    relay_to = jnp.where(me == 0, 15, jnp.where(me == 5, 11, jnp.where(me == 10, 9, 13)))
     is_far = me >= 8
     owns_far = (me >= 4) & (me < 12)
 
@@ -89,7 +89,8 @@
     greet((me == 10) | (me == 11), 5)
     greet(me == 5, 6)
     greet(me == 8, 10)
-    greet(me == 9, 14)
+    greet(me == 9, 15)
+    greet((me == 12) | (me == 13), 14)
     greet(me == 0, 11)
     greet((me == 14) | (me == 15), 0)
 
@@ -104,14 +105,14 @@
         load.start()
 
     expected = has_right.astype(jnp.int32)
-    for device, more in ((0, 2), (5, 2), (6, 1), (10, 1), (11, 1), (14, 1)):
+    for device, more in ((0, 2), (5, 2), (6, 1), (10, 1), (11, 1), (14, 2), (15, 1)):
         expected += jnp.where(me == device, more, 0)
 
-    @pl.when(has_right)
+    @pl.when(me != FIRST - 1)
     def _():
         pl.semaphore_wait(barrier, expected)
 
-    @pl.when(me == 14)
+    @pl.when(me == 15)
     def _():
         pl.semaphore_signal(far_ready, inc=1, device_id={"ctx": 9}, device_id_type=MESH)
 
@@ -154,8 +155,8 @@
         def _():
             forward(k, c).start()
 
-    def relay(c):
-        @pl.when(is_relay)
+    def relay(c, condition):
+        @pl.when(is_relay & condition)
         def _():
             to_relay(c).wait_recv()
             for which in (1, 0):
@@ -263,8 +264,9 @@
     first, second = range(PIECES), range(PIECES, CHUNKS)
     when_reached(1, lambda: scores(1))
     for c in range(CHUNKS):
+        relay(c, me != 10)
         when_reached(2, arrive(2, c))
-        relay(c)
+        relay(c, me == 10)
     when_reached(1, lambda: grad_dots(1))
     when_reached(2, lambda: scores(2))
     when_reached(3, *[arrive(3, c) for c in first], lambda: scores(3))

time: 36.4 us -> 35.9 us (0.986)
  no operation moved by 1% of the time
where the time goes in v7:
time: 35.9 us; the launch traced here: 35.6 us
  Pallas kernels  34.9 us (97%)
  between operations  0.64 us (2%)
    pallas_call x1, Pallas kernels, shards(): pl.pallas_call(attention_kernel, out_shape=results, in_specs=[in_hbm] * 5...  34.1 us
    pallas_call x1, Pallas kernels, shards(): pl.pallas_call(store_kernel, out_shape=results, in_specs=[in_vmem] * 3, o...  0.85 us

profile of v7, /device:TPU:22, one launch (start us, length us, event | category | flops | bytes accessed | tf_op | source)
XLA Modules:
  0.0 35.6 jit_solution(9602852140618779051)
XLA Ops:
  0.6 34.1 %shard_map.76 = (bf16[256,1024]{1,0:T(8,128)(2,1)S(1)}, bf16[256,128]{1,0:T(8,128)(2,1)S(1)}, bf16[256,128]{1,0:T(8,128)(2,1)S(1)}) custom-call(s32[16]{0:T(128)} %lengths_hbm.1, bf16[256,1024]{1,0:T(8,128)(2,1)} %q_hbm.1, bf16[256,128]{1,0:T(8,128)(2,1)} %k_hbm.1, bf16[256,128]{1,0:T(8,128)(2,1)} %v_hbm.1, bf16[256,1024]{1,0:T(8,128)(2,1)} %o_hbm.1), custom_call_target="tpu_custom_call" | custom-call | tf_op jit(solution)/shard_map/pallas_call | solution.py:458
  34.7 0.9 %shard_map.77 = (bf16[256,1024]{1,0:T(8,128)(2,1)}, bf16[256,128]{1,0:T(8,128)(2,1)}, bf16[256,128]{1,0:T(8,128)(2,1)}) custom-call(bf16[256,1024]{1,0:T(8,128)(2,1)S(1)} %get-tuple-element.6.dq, bf16[256,128]{1,0:T(8,128)(2,1)S(1)} %get-tuple-element.7.dk, bf16[256,128]{1,0:T(8,128)(2,1)S(1)} %get-tuple-element.8.dv), custom_call_target="tpu_custom_call" | custom-call | tf_op jit(solution)/shard_map/pallas_call | solution.py:501

commit v8 on v7

--- a/solution.py
+++ b/solution.py
@@ -386,11 +386,9 @@
         when_reached(2, *passed(2, chunks))
     when_reached(1, lambda: gradients(1))
     when_reached(1, *passed(1, range(CHUNKS)))
-    for c in first:
+    for c in range(CHUNKS):
         pass_far(c)
     gradients(0)
-    for c in second:
-        pass_far(c)
     for h in range(HEADS):
         dq_out[:, h * WIDTH : (h + 1) * WIDTH] = (dq_acc[h] * score_scale).T.astype(jnp.bfloat16)
 

time: 35.9 us -> 35.7 us (level)
  no operation moved by 1% of the time
where the time goes in v8:
time: 35.7 us; the launch traced here: 35.6 us
  Pallas kernels  34.9 us (98%)
  between operations  0.64 us (2%)
    pallas_call x1, Pallas kernels, shards(): pl.pallas_call(attention_kernel, out_shape=results, in_specs=[in_hbm] * 5...  34.1 us
    pallas_call x1, Pallas kernels, shards(): pl.pallas_call(store_kernel, out_shape=results, in_specs=[in_vmem] * 3, o...  0.85 us

profile of v8, /device:TPU:22, one launch (start us, length us, event | category | flops | bytes accessed | tf_op | source)
XLA Modules:
  0.0 35.6 jit_solution(7616664522032549994)
XLA Ops:
  0.6 34.1 %shard_map.76 = (bf16[256,1024]{1,0:T(8,128)(2,1)S(1)}, bf16[256,128]{1,0:T(8,128)(2,1)S(1)}, bf16[256,128]{1,0:T(8,128)(2,1)S(1)}) custom-call(s32[16]{0:T(128)} %lengths_hbm.1, bf16[256,1024]{1,0:T(8,128)(2,1)} %q_hbm.1, bf16[256,128]{1,0:T(8,128)(2,1)} %k_hbm.1, bf16[256,128]{1,0:T(8,128)(2,1)} %v_hbm.1, bf16[256,1024]{1,0:T(8,128)(2,1)} %o_hbm.1), custom_call_target="tpu_custom_call" | custom-call | tf_op jit(solution)/shard_map/pallas_call | solution.py:456
  34.7 0.9 %shard_map.77 = (bf16[256,1024]{1,0:T(8,128)(2,1)}, bf16[256,128]{1,0:T(8,128)(2,1)}, bf16[256,128]{1,0:T(8,128)(2,1)}) custom-call(bf16[256,1024]{1,0:T(8,128)(2,1)S(1)} %get-tuple-element.6.dq, bf16[256,128]{1,0:T(8,128)(2,1)S(1)} %get-tuple-element.7.dk, bf16[256,128]{1,0:T(8,128)(2,1)S(1)} %get-tuple-element.8.dv), custom_call_target="tpu_custom_call" | custom-call | tf_op jit(solution)/shard_map/pallas_call | solution.py:499

commit v9 on v8

--- a/solution.py
+++ b/solution.py
@@ -126,7 +126,7 @@
 
     def own_piece(c):
         part, rows = piece(c)
-        return (k_hbm, v_hbm)[part].at[rows]
+        return (keys, values)[part].at[0, rows]
 
     def forward(k, c):
         part, rows = piece(c)
@@ -162,6 +162,8 @@
             for which in (1, 0):
                 from_relay(c, which).start()
 
+    loads[1].wait()
+    loads[2].wait()
     for c in range(CHUNKS):
         send_forward(0, c)
 
@@ -247,10 +249,8 @@
 
         to_relay(c).start()
 
-    loads[1].wait()
     loads[3].wait()
     scores(0)
-    loads[2].wait()
     loads[4].wait()
     grad_dots(0)
 

time: 35.7 us -> 35.6 us (level)
  no operation moved by 1% of the time
where the time goes in v9:
time: 35.6 us; the launch traced here: 35.5 us
  Pallas kernels  34.8 us (98%)
  between operations  0.64 us (2%)
    pallas_call x1, Pallas kernels, shards(): pl.pallas_call(attention_kernel, out_shape=results, in_specs=[in_hbm] * 5...  34 us
    pallas_call x1, Pallas kernels, shards(): pl.pallas_call(store_kernel, out_shape=results, in_specs=[in_vmem] * 3, o...  0.85 us

profile of v9, /device:TPU:22, one launch (start us, length us, event | category | flops | bytes accessed | tf_op | source)
XLA Modules:
  0.0 35.5 jit_solution(1360559763119883111)
XLA Ops:
  0.6 34.0 %shard_map.76 = (bf16[256,1024]{1,0:T(8,128)(2,1)S(1)}, bf16[256,128]{1,0:T(8,128)(2,1)S(1)}, bf16[256,128]{1,0:T(8,128)(2,1)S(1)}) custom-call(s32[16]{0:T(128)} %lengths_hbm.1, bf16[256,1024]{1,0:T(8,128)(2,1)} %q_hbm.1, bf16[256,128]{1,0:T(8,128)(2,1)} %k_hbm.1, bf16[256,128]{1,0:T(8,128)(2,1)} %v_hbm.1, bf16[256,1024]{1,0:T(8,128)(2,1)} %o_hbm.1), custom_call_target="tpu_custom_call" | custom-call | tf_op jit(solution)/shard_map/pallas_call | solution.py:456
  34.6 0.9 %shard_map.77 = (bf16[256,1024]{1,0:T(8,128)(2,1)}, bf16[256,128]{1,0:T(8,128)(2,1)}, bf16[256,128]{1,0:T(8,128)(2,1)}) custom-call(bf16[256,1024]{1,0:T(8,128)(2,1)S(1)} %get-tuple-element.6.dq, bf16[256,128]{1,0:T(8,128)(2,1)S(1)} %get-tuple-element.7.dk, bf16[256,128]{1,0:T(8,128)(2,1)S(1)} %get-tuple-element.8.dv), custom_call_target="tpu_custom_call" | custom-call | tf_op jit(solution)/shard_map/pallas_call | solution.py:499
